TPU v7x, 128 devices: a whole 4x4x4 slice. The times are simulated.
128 devices in a mesh: dp: 8 (over x, core), group: 16 (over z, y).
Axes of the slice: x: 4, y: 4, z: 4, core: 2. Of those that a mesh axis runs over, the one named last changes fastest.
Arguments:
- query_first: bfloat16 [131072, 256], P(('dp', 'group')), may hold values from -400 to 400
- query_second: bfloat16 [131072, 512], P(('dp', 'group')), may hold values from -400 to 400
- query_third: bfloat16 [131072, 1024], P(('dp', 'group')), may hold values from -400 to 400
- passage_first: bfloat16 [131072, 256], P(('dp', 'group')), may hold values from -400 to 400
- passage_second: bfloat16 [131072, 512], P(('dp', 'group')), may hold values from -400 to 400
- passage_third: bfloat16 [131072, 1024], P(('dp', 'group')), may hold values from -400 to 400
- neg_blocks: int32 [512, 127], P(('dp', 'group')), may hold values from -1 to 16383, as said below
- positives: int32 [131072], P(('dp', 'group')), may hold values from 0 to 131071, as said below
Outputs:
- losses: float32 [131072], P(('dp', 'group'))
- grad_query_first: float32 [131072, 256], P(('dp', 'group'))
- grad_query_second: float32 [131072, 512], P(('dp', 'group'))
- grad_query_third: float32 [131072, 1024], P(('dp', 'group'))
- grad_passage_first: float32 [131072, 256], P(('dp', 'group'))
- grad_passage_second: float32 [131072, 512], P(('dp', 'group'))
- grad_passage_third: float32 [131072, 1024], P(('dp', 'group'))
Inputs may be any that keep to these rules, and one draw needn't show every extreme that they name: `neg_blocks`: row b lists hard-negative blocks of query block b (queries b * 256 to (b + 1) * 256 - 1). Block k is the passage rows k * 8 to (k + 1) * 8 - 1 and lies on device k // 128 in the order of dp+group. A row holds a quarter of 127 (rounded down) to 127 distinct block ids first and -1 after them; some row holds 127. No row names a block of its own query block's device. Over all rows of one device, the named blocks that lie on any one other device are one and the same block. `positives`: the positive of a query is a passage row of the query's own device; every passage row is the positive of exactly one query.
All inputs are finite; a program needn't handle non-finite values.
Results may differ from a plain program's by a relative error of at most 0.0041.
Values may be sent and summed in bfloat16 or wider, within the bound.
No kernel may reach another device: no remote copies, remote signals or barrier semaphores. Data moves between devices by JAX's collectives and lax.ppermute only.
A program may use at most 128 MiB of HBM per device.

v0:
```python
import functools
import math

import jax
import jax.numpy as jnp
from jax import lax
from jax.experimental import pallas as pl
from jax.experimental.pallas import tpu as pltpu
from jax.sharding import PartitionSpec as P

PROWS = 8
LANES = 128
AXES = ("dp", "group")

EPSILON = 1e-06
SHARPNESS = 20.0
EXP_SCALE = SHARPNESS * math.log2(math.e)
OFF = -1e30

F32 = jnp.float32
BF16 = jnp.bfloat16
ANY = pl.BlockSpec(memory_space=pl.ANY)
VMEM = pl.BlockSpec(memory_space=pltpu.VMEM)
SMEM = pl.BlockSpec(memory_space=pltpu.SMEM)
MIB = 1024 * 1024
NT = (((1,), (1,)), ((), ()))
TN = (((0,), (0,)), ((), ()))
NN = (((1,), (0,)), ((), ()))


def exchange(values):
    return lax.all_to_all(values, AXES, split_axis=0, concat_axis=0, tiled=True)


def cost(flops, moved):
    return pl.CostEstimate(flops=int(flops), bytes_accessed=int(moved), transcendentals=0)


def columns_of(widths):
    starts = {}
    at = 0
    for index in sorted(range(len(widths)), key=lambda i: -widths[i]):
        starts[index] = at
        at += widths[index]
    return [starts[i] for i in range(len(widths))]


def wanted_kernel(block_count, neg_ref, out_ref):
    peers = out_ref.shape[0]
    lists, entries = neg_ref.shape
    peer = lax.broadcasted_iota(jnp.int32, (peers, entries), 0)
    best = jnp.full((peers, 1), -1, jnp.int32)
    for row in range(lists):
        ids = jnp.broadcast_to(neg_ref[row : row + 1, :], (peers, entries))
        local_ids = ids - peer * block_count
        hit = (local_ids >= 0) & (local_ids < block_count)
        best = jnp.maximum(best, jnp.max(jnp.where(hit, local_ids, -1), axis=1, keepdims=True))
    out_ref[...] = jnp.broadcast_to(best, out_ref.shape)


def heads_kernel(widths, starts, *refs):
    raws, (q_out, p_out, inv_out) = refs[:6], refs[6:]
    lane = lax.broadcasted_iota(jnp.int32, inv_out.shape, 1)
    packed = jnp.zeros(inv_out.shape, F32)
    for side, out in enumerate((q_out, p_out)):
        for k in range(3):
            values = raws[side * 3 + k][...].astype(F32)
            inverse = lax.rsqrt(jnp.sum(values * values, axis=1, keepdims=True) + EPSILON)
            out[:, starts[k] : starts[k] + widths[k]] = (values * inverse).astype(BF16)
            packed = jnp.where(lane == side * 3 + k, inverse, packed)
    inv_out[...] = packed


def gather_kernel(pairs, asked_ref, p_ref, out_ref):
    base = pl.program_id(0) * pairs

    def block(peer):
        ident = jnp.maximum(asked_ref[peer, 0], 0)
        start = pl.multiple_of((ident // 2) * 16, 16)
        both = p_ref[pl.ds(start, 16), :].astype(F32)
        return jnp.where(ident % 2 == 0, both[:8], both[8:])

    for pair in range(pairs):
        peer = (base + pair) * 2
        rows = jnp.concatenate([block(peer), block(peer + 1)], axis=0)
        out_ref[pair * 16 : pair * 16 + 16, :] = rows.astype(BF16)


def local_kernel(widths, starts, block_count, p_ref, q_ref, pos_ref, neg_ref, tot_ref, spos_ref, bias_ref):
    rows = p_ref.shape[0]
    cols = q_ref.shape[0]
    chunk = min(256, rows)
    pos = pos_ref[0:1, :]
    for k in range(3):
        span = slice(starts[k], starts[k] + widths[k])
        q = q_ref[:, span]
        tot = jnp.zeros((1, cols), F32)
        spos = jnp.zeros((1, cols), F32)
        for at in range(0, rows, chunk):
            s = lax.dot_general(p_ref[at : at + chunk, span], q, NT, preferred_element_type=F32)
            row = lax.broadcasted_iota(jnp.int32, (chunk, cols), 0) + at
            tot = tot + jnp.sum(jnp.exp2(s * EXP_SCALE), axis=0, keepdims=True)
            spos = spos + jnp.sum(jnp.where(row == pos, s, 0.0), axis=0, keepdims=True)
        tot_ref[k : k + 1, :] = tot
        spos_ref[k : k + 1, :] = spos * SHARPNESS
    far = bias_ref.shape[0]
    entries = neg_ref.shape[2]
    peer = lax.broadcasted_iota(jnp.int32, (far, entries), 0) // PROWS
    local_ids = jnp.broadcast_to(neg_ref[0], (far, entries)) - peer * block_count
    hit = (local_ids >= 0) & (local_ids < block_count)
    listed = jnp.max(jnp.where(hit, 1.0, 0.0), axis=1, keepdims=True)
    bias_ref[...] = jnp.broadcast_to(jnp.where(listed > 0.0, 0.0, OFF), bias_ref.shape)


def far_kernel(
    widths, starts, lists, far_any, q_any, bias_ref, tot_ref, spos_ref,
    term_any, g_any, scale_ref, loss_ref,
    far_v, q_v, e_v, g_v, term_v, in_sems, g_sems, term_sems,
):
    far, rows = g_v.shape[1], g_v.shape[2]
    cols = rows // lists
    chunk = min(256, far)
    order = (0, 1, 2)
    loads = {}
    for k in order:
        span = pl.ds(starts[k], widths[k])
        loads[k] = (
            pltpu.make_async_copy(far_any.at[:, span], far_v.at[:, span], in_sems.at[k, 0]),
            pltpu.make_async_copy(q_any.at[:, span], q_v.at[:, span], in_sems.at[k, 1]),
        )
        for load in loads[k]:
            load.start()
    stores = []
    loss = jnp.zeros((1, rows), F32)
    for k in order:
        span = slice(starts[k], starts[k] + widths[k])
        for load in loads[k]:
            load.wait()
        for b in range(lists):
            at_q = slice(b * cols, (b + 1) * cols)
            q = q_v[at_q, span]
            tot = tot_ref[k : k + 1, at_q]
            for at in range(0, far, chunk):
                s = lax.dot_general(far_v[at : at + chunk, span], q, NT, preferred_element_type=F32)
                bias = bias_ref[at : at + chunk, b * LANES : b * LANES + 1]
                e = jnp.exp2(s * EXP_SCALE + bias)
                tot = tot + jnp.sum(e, axis=0, keepdims=True)
                e_v[at : at + chunk, at_q] = e
            scale = SHARPNESS / tot
            scale_ref[k : k + 1, at_q] = scale
            loss_ref[k : k + 1, at_q] = jnp.log(tot) - spos_ref[k : k + 1, at_q]
            for at in range(0, far, chunk):
                g_v[k, at : at + chunk, at_q] = (e_v[at : at + chunk, at_q] * scale).astype(BF16)
        store = pltpu.make_async_copy(g_v.at[k], g_any.at[k], g_sems.at[k])
        store.start()
        stores.append(store)
        step = 256
        for at in range(0, widths[k], step):
            here = slice(starts[k] + at, starts[k] + at + step)
            for row in range(0, far, chunk):
                part = jnp.dot(g_v[k, row : row + chunk, :], q_v[:, here], preferred_element_type=F32)
                term_v[row : row + chunk, here] = part.astype(BF16)
        store = pltpu.make_async_copy(
            term_v.at[:, pl.ds(starts[k], widths[k])],
            term_any.at[:, pl.ds(starts[k], widths[k])],
            term_sems.at[k],
        )
        store.start()
        stores.append(store)
    for store in stores:
        store.wait()


def near_kernel(
    k, p_ref, q_ref, far_ref, g_ref, raw_ref, inv_ref, scale_ref, pos_ref, out_ref, dp_ref
):
    rows = p_ref.shape[0]
    cols = q_ref.shape[0]
    q = q_ref[...]
    pos = pos_ref[0:1, :]
    scale = scale_ref[k : k + 1, :]
    chunk = min(256, rows)
    first = pl.program_id(0) == 0
    dq = lax.dot_general(g_ref[0], far_ref[...], TN, preferred_element_type=F32)
    parts = []
    for at in range(0, rows, chunk):
        s = lax.dot_general(p_ref[at : at + chunk, :], q, NT, preferred_element_type=F32)
        row = lax.broadcasted_iota(jnp.int32, (chunk, cols), 0) + at
        g = jnp.exp2(s * EXP_SCALE) * scale
        parts.append((g - jnp.where(row == pos, SHARPNESS, 0.0)).astype(BF16))
    weights = jnp.concatenate(parts, axis=0)
    dq = dq + lax.dot_general(weights, p_ref[...], TN, preferred_element_type=F32)
    dp = jnp.dot(weights, q, preferred_element_type=F32)

    @pl.when(first)
    def _():
        dp_ref[...] = dp

    @pl.when(jnp.logical_not(first))
    def _():
        dp_ref[...] += dp

    inverse = inv_ref[:, k : k + 1]
    unit = raw_ref[...].astype(F32) * inverse
    out_ref[...] = (dq - unit * jnp.sum(unit * dq, axis=1, keepdims=True)) * inverse


def passage_kernel(
    widths, starts, asked_ref, term_any, dp0, dp1, dp2, raw0, raw1, raw2, inv_ref,
    out0, out1, out2,
    term_v, acc0, acc1, acc2, rv0, rv1, rv2, in_sems, out_sems,
):
    dps, raws, outs = (dp0, dp1, dp2), (raw0, raw1, raw2), (out0, out1, out2)
    accs, raw_vs = (acc0, acc1, acc2), (rv0, rv1, rv2)
    rows = acc0.shape[0]
    peers = term_v.shape[0] // PROWS
    order = (0, 1, 2)
    loads = {}
    for k in order:
        span = pl.ds(starts[k], widths[k])
        loads[k] = (
            pltpu.make_async_copy(term_any.at[:, span], term_v.at[:, span], in_sems.at[k, 0]),
            pltpu.make_async_copy(dps[k], accs[k], in_sems.at[k, 1]),
            pltpu.make_async_copy(raws[k], raw_vs[k], in_sems.at[k, 2]),
        )
        for load in loads[k]:
            load.start()
    stores = []
    chunk = rows // 4
    for k in order:
        for load in loads[k]:
            load.wait()
        acc, raw = accs[k], raw_vs[k]
        span = pl.ds(starts[k], widths[k])

        def add(pair, carry):
            both = term_v[pl.ds(pl.multiple_of(pair * 16, 16), 16), span].astype(F32)
            for half in range(2):
                ident = jnp.maximum(asked_ref[pair * 2 + half, 0], 0)
                place = pl.ds(pl.multiple_of(ident * PROWS, PROWS), PROWS)
                acc[place, :] = acc[place, :] + both[half * 8 : half * 8 + 8]
            return carry

        lax.fori_loop(0, peers // 2, add, 0)
        for c in range(4):
            def finish(step, carry):
                place = pl.ds(pl.multiple_of(c * chunk + step * 32, 32), 32)
                inverse = inv_ref[place, 3 + k : 4 + k]
                unit = raw[place, :].astype(F32) * inverse
                dp = acc[place, :]
                dot = jnp.sum(unit * dp, axis=1, keepdims=True)
                acc[place, :] = (dp - unit * dot) * inverse
                return carry

            lax.fori_loop(0, chunk // 32, finish, 0)
            part = pl.ds(c * chunk, chunk)
            store = pltpu.make_async_copy(acc.at[part, :], outs[k].at[part, :], out_sems.at[k, c])
            store.start()
            stores.append(store)
    for store in stores:
        store.wait()


def local(
    query_first, query_second, query_third,
    passage_first, passage_second, passage_third,
    neg_blocks, positives,
):
    devices = lax.axis_size(AXES)
    own = lax.axis_index(AXES)
    queries = (query_first, query_second, query_third)
    passages = (passage_first, passage_second, passage_third)
    widths = [values.shape[1] for values in queries]
    starts = columns_of(widths)
    wide = sum(widths)
    rows = query_first.shape[0]
    block_count = rows // PROWS
    lists, entries = neg_blocks.shape
    far = devices * PROWS
    cols = rows // lists
    params = functools.partial(pltpu.CompilerParams)

    wanted = pl.pallas_call(
        functools.partial(wanted_kernel, block_count),
        out_shape=jax.ShapeDtypeStruct((devices, LANES), jnp.int32),
        in_specs=[VMEM],
        out_specs=VMEM,
    )(neg_blocks)
    asked = exchange(wanted[:, None, :]).reshape(devices, LANES)

    step = rows // 8
    row_block = lambda width: pl.BlockSpec((step, width), lambda i: (i, 0))
    q_all, p_all, inverses = pl.pallas_call(
        functools.partial(heads_kernel, widths, starts),
        grid=(8,),
        out_shape=(
            jax.ShapeDtypeStruct((rows, wide), BF16),
            jax.ShapeDtypeStruct((rows, wide), BF16),
            jax.ShapeDtypeStruct((rows, LANES), F32),
        ),
        in_specs=[row_block(width) for width in widths + widths],
        out_specs=(row_block(wide), row_block(wide), row_block(LANES)),
        compiler_params=params(vmem_limit_bytes=24 * MIB),
        cost_estimate=cost(rows * wide * 8, rows * wide * 8),
    )(*queries, *passages)

    pairs = max(1, devices // 2 // 8)
    send = pl.pallas_call(
        functools.partial(gather_kernel, pairs),
        grid=(devices // 2 // pairs,),
        out_shape=jax.ShapeDtypeStruct((far, wide), BF16),
        in_specs=[SMEM, pl.BlockSpec((rows, wide), lambda i: (0, 0))],
        out_specs=pl.BlockSpec((pairs * 16, wide), lambda i: (i, 0)),
        compiler_params=params(vmem_limit_bytes=24 * MIB),
        cost_estimate=cost(far * wide, far * wide * 4),
    )(asked, p_all)
    fetched = exchange(send.reshape(devices, PROWS, wide)).reshape(far, wide)

    local_pos = (positives - own * rows).reshape(1, rows)
    whole = lambda shape: pl.BlockSpec(shape, lambda i: (0,) * len(shape))
    lane_block = pl.BlockSpec((8, cols), lambda i: (0, i))
    pos_block = pl.BlockSpec((1, cols), lambda i: (0, i))
    totals, positive_scores, bias = pl.pallas_call(
        functools.partial(local_kernel, widths, starts, block_count),
        grid=(lists,),
        out_shape=(
            jax.ShapeDtypeStruct((8, rows), F32),
            jax.ShapeDtypeStruct((8, rows), F32),
            jax.ShapeDtypeStruct((far, lists * LANES), F32),
        ),
        in_specs=[
            whole((rows, wide)),
            pl.BlockSpec((cols, wide), lambda i: (i, 0)),
            pos_block,
            pl.BlockSpec((1, 1, entries), lambda i: (i, 0, 0)),
        ],
        out_specs=(lane_block, lane_block, pl.BlockSpec((far, LANES), lambda i: (0, i))),
        compiler_params=params(vmem_limit_bytes=32 * MIB),
        cost_estimate=cost(2 * rows * rows * wide, rows * wide * 4),
    )(p_all, q_all, local_pos, neg_blocks.reshape(lists, 1, entries))

    terms, far_weights, scales, loss_rows = pl.pallas_call(
        functools.partial(far_kernel, widths, starts, lists),
        out_shape=(
            jax.ShapeDtypeStruct((far, wide), BF16),
            jax.ShapeDtypeStruct((3, far, rows), BF16),
            jax.ShapeDtypeStruct((8, rows), F32),
            jax.ShapeDtypeStruct((8, rows), F32),
        ),
        in_specs=[ANY, ANY, VMEM, VMEM, VMEM],
        out_specs=(ANY, ANY, VMEM, VMEM),
        scratch_shapes=[
            pltpu.VMEM((far, wide), BF16),
            pltpu.VMEM((rows, wide), BF16),
            pltpu.VMEM((far, rows), F32),
            pltpu.VMEM((3, far, rows), BF16),
            pltpu.VMEM((far, wide), BF16),
            pltpu.SemaphoreType.DMA((3, 2)),
            pltpu.SemaphoreType.DMA((3,)),
            pltpu.SemaphoreType.DMA((3,)),
        ],
        compiler_params=params(vmem_limit_bytes=40 * MIB),
        cost_estimate=cost(4 * far * rows * wide, 6 * far * wide),
    )(fetched, q_all, bias, totals, positive_scores)
    losses = loss_rows[0] + loss_rows[1] + loss_rows[2]
    returned = exchange(terms.reshape(devices, PROWS, wide)).reshape(far, wide)

    q_grads = []
    dp_parts = []
    for k in range(3):
        width = widths[k]
        place = starts[k] // width
        q_grad, dp_part = pl.pallas_call(
            functools.partial(near_kernel, k),
            grid=(lists,),
            out_shape=(
                jax.ShapeDtypeStruct((rows, width), F32),
                jax.ShapeDtypeStruct((rows, width), F32),
            ),
            in_specs=[
                pl.BlockSpec((rows, width), lambda i, place=place: (0, place)),
                pl.BlockSpec((cols, width), lambda i, place=place: (i, place)),
                pl.BlockSpec((far, width), lambda i, place=place: (0, place)),
                pl.BlockSpec((1, far, cols), lambda i, k=k: (k, 0, i)),
                pl.BlockSpec((cols, width), lambda i: (i, 0)),
                pl.BlockSpec((cols, LANES), lambda i: (i, 0)),
                lane_block,
                pos_block,
            ],
            out_specs=(
                pl.BlockSpec((cols, width), lambda i: (i, 0)),
                pl.BlockSpec((rows, width), lambda i: (0, 0)),
            ),
            compiler_params=params(vmem_limit_bytes=40 * MIB),
            cost_estimate=cost(8 * rows * rows * width, 16 * rows * width),
        )(p_all, q_all, fetched, far_weights, queries[k], inverses, scales, local_pos)
        q_grads.append(q_grad)
        dp_parts.append(dp_part)

    p_grads = pl.pallas_call(
        functools.partial(passage_kernel, widths, starts),
        out_shape=tuple(jax.ShapeDtypeStruct((rows, width), F32) for width in widths),
        in_specs=[SMEM] + [ANY] * 7 + [VMEM],
        out_specs=(ANY, ANY, ANY),
        scratch_shapes=[pltpu.VMEM((far, wide), BF16)]
        + [pltpu.VMEM((rows, width), F32) for width in widths]
        + [pltpu.VMEM((rows, width), BF16) for width in widths]
        + [pltpu.SemaphoreType.DMA((3, 3)), pltpu.SemaphoreType.DMA((3, 4))],
        compiler_params=params(vmem_limit_bytes=32 * MIB),
        cost_estimate=cost(16 * rows * wide, 12 * rows * wide),
    )(asked, returned, *dp_parts, *passages, inverses)
    return (losses, *q_grads, *p_grads)


def solution(mesh):
    rows = P(AXES, None)
    return jax.shard_map(
        local,
        mesh=mesh,
        in_specs=(rows,) * 7 + (P(AXES),),
        out_specs=(P(AXES),) + (rows,) * 6,
        check_vma=False,
    )
```

profile of v0, /device:TPU:1, one launch (start us, length us, event | category | flops | bytes accessed | tf_op | source)
XLA Modules:
  0.0 186.2 jit_solution(6408519999337206210)
XLA Ops:
  0.6 1.6 shard_map.135
  2.2 11.5 %all-to-all-start = ((s32[128,1,128]{2,1,0:T(1,128)}), s32[128,1,128]{2,1,0:T(1,128)S(1)}, u32[]{:S(2)}, u32[]{:S(2)}) async-start(s32[128,1,128]{2,1,0:T(1,128)} %bitcast.20), calls=%async_computation | async-start | bytes 131072 | tf_op jit(solution)/shard_map/all_to_all | solution.py:32
  13.8 1.6 copy-done.10
  15.3 1.2 copy-done.13
  18.8 1.6 copy-done.20
  21.5 2.5 %shard_map.136 = (bf16[1024,1792]{1,0:T(8,128)(2,1)S(1)}, bf16[1024,1792]{1,0:T(8,128)(2,1)S(1)}, f32[1024,128]{1,0:T(8,128)S(1)}) custom-call(bf16[1024,256]{1,0:T(8,128)(2,1)S(1)} %copy-done.18, bf16[1024,512]{1,0:T(8,128)(2,1)S(1)} %copy-done.13, bf16[1024,1024]{1,0:T(8,128)(2,1)S(1)} %copy-done.20, bf16[1024,256]{1,0:T(8,128)(2,1)S(1)} %copy-done.24, ...), custom_call_target="tpu_custom_call" | custom-call | flops 14680064 | bytes 14680064 | tf_op jit(solution)/shard_map/pallas_call | solution.py:293
  24.0 1.8 copy-done
  25.9 1.8 copy-done.6
  27.7 2.0 %copy-done.1 = bf16[1024,1792]{1,0:T(8,128)(2,1)S(1)} copy-done((bf16[1024,1792]{1,0:T(8,128)(2,1)S(1)}, bf16[1024,1792]{1,0:T(8,128)(2,1)}, u32[]{:S(2)}) %copy-start.1) | copy-done | bytes 3670040
  29.7 2.7 %shard_map.137 = bf16[1024,1792]{1,0:T(8,128)(2,1)S(1)} custom-call(s32[128,128]{1,0:T(8,128)S(1)} %bitcast.13, bf16[1024,1792]{1,0:T(8,128)(2,1)S(1)} %copy-done.1), custom_call_target="tpu_custom_call" | custom-call | flops 1835008 | bytes 7340032 | tf_op jit(solution)/shard_map/pallas_call | solution.py:308
  32.4 1.8 copy-done.5
  34.3 10.2 %all-to-all-start.1 = ((bf16[128,8,1792]{2,1,0:T(8,128)(2,1)}), bf16[128,8,1792]{2,1,0:T(8,128)(2,1)}, u32[]{:S(2)}, u32[]{:S(2)}) async-start(bf16[128,8,1792]{2,1,0:T(8,128)(2,1)} %bitcast.11), calls=%async_computation.1 | async-start | bytes 7340032 | tf_op jit(solution)/shard_map/all_to_all | solution.py:32
  44.5 2.0 %copy-done.2 = bf16[1024,1792]{1,0:T(8,128)(2,1)S(1)} copy-done((bf16[1024,1792]{1,0:T(8,128)(2,1)S(1)}, bf16[1024,1792]{1,0:T(8,128)(2,1)}, u32[]{:S(2)}) %copy-start.2) | copy-done | bytes 3670040
  46.5 2.0 %copy-done.7 = bf16[1024,1792]{1,0:T(8,128)(2,1)S(1)} copy-done((bf16[1024,1792]{1,0:T(8,128)(2,1)S(1)}, bf16[1024,1792]{1,0:T(8,128)(2,1)}, u32[]{:S(2)}) %copy-start.7) | copy-done | bytes 3670040
  48.6 5.5 %shard_map.138 = (f32[8,1024]{1,0:T(8,128)S(1)}, f32[8,1024]{1,0:T(8,128)S(1)}, f32[1024,512]{1,0:T(8,128)S(1)}) custom-call(bf16[1024,1792]{1,0:T(8,128)(2,1)S(1)} %copy-done.2, bf16[1024,1792]{1,0:T(8,128)(2,1)S(1)} %copy-done.7, s32[1,1024]{1,0:T(1,128)S(1)} %bitcast.15, s32[4,1,127]{2,1,0:T(1,128)S(1)} %bitcast.19), custom_call_target="tpu_custom_call" | custom-call | flops 3758096384 | bytes 7340032 | tf_op jit(solution)/shard_map/pallas_call | solution.py:323
  54.0 1.3 copy-done.29
  55.4 34.9 %all-to-all-done.1 = bf16[128,8,1792]{2,1,0:T(8,128)(2,1)} async-done(((bf16[128,8,1792]{2,1,0:T(8,128)(2,1)}), bf16[128,8,1792]{2,1,0:T(8,128)(2,1)}, u32[]{:S(2)}, u32[]{:S(2)}) %all-to-all-start.1) | async-done | bytes 3670048 | tf_op jit(solution)/shard_map/all_to_all | solution.py:32
  90.3 2.0 %copy-done.8 = bf16[1024,1792]{1,0:T(8,128)(2,1)S(1)} copy-done((bf16[1024,1792]{1,0:T(8,128)(2,1)S(1)}, bf16[1024,1792]{1,0:T(8,128)(2,1)}, u32[]{:S(2)}) %copy-start.8) | copy-done | bytes 3670040
  92.3 1.6 copy-done.30
  93.9 10.4 %shard_map.139 = (bf16[1024,1792]{1,0:T(8,128)(2,1)S(1)}, bf16[3,1024,1024]{2,1,0:T(8,128)(2,1)}, f32[8,1024]{1,0:T(8,128)S(1)}, f32[8,1024]{1,0:T(8,128)S(1)}) custom-call(bf16[1024,1792]{1,0:T(8,128)(2,1)} %bitcast.4.far_any.far_ref, bf16[1024,1792]{1,0:T(8,128)(2,1)S(1)} %copy-done.8, f32[1024,512]{1,0:T(8,128)S(1)} %copy-done.30, ...), custom_call_target="tpu_custom_call" | custom-call | flops 7516192768 | bytes 11010048 | tf_op jit(solution)/shard_map/pallas_call | solution.py:342
  104.3 1.8 copy-done.17
  106.1 5.7 %all-to-all-start.2 = ((bf16[128,8,1792]{2,1,0:T(8,128)(2,1)}), bf16[128,8,1792]{2,1,0:T(8,128)(2,1)}, u32[]{:S(2)}, u32[]{:S(2)}) async-start(bf16[128,8,1792]{2,1,0:T(8,128)(2,1)} %bitcast.12), calls=%async_computation.2 | async-start | bytes 7340032 | tf_op jit(solution)/shard_map/all_to_all | solution.py:32
  111.8 2.0 %copy-done.3 = bf16[1024,1792]{1,0:T(8,128)(2,1)S(1)} copy-done((bf16[1024,1792]{1,0:T(8,128)(2,1)S(1)}, bf16[1024,1792]{1,0:T(8,128)(2,1)}, u32[]{:S(2)}) %copy-start.3) | copy-done | bytes 3670040
  113.9 2.0 %copy-done.9 = bf16[1024,1792]{1,0:T(8,128)(2,1)S(1)} copy-done((bf16[1024,1792]{1,0:T(8,128)(2,1)S(1)}, bf16[1024,1792]{1,0:T(8,128)(2,1)}, u32[]{:S(2)}) %copy-start.9) | copy-done | bytes 3670040
  115.9 7.2 %shard_map.140 = (f32[1024,256]{1,0:T(8,128)}, f32[1024,256]{1,0:T(8,128)S(1)}) custom-call(bf16[1024,1792]{1,0:T(8,128)(2,1)S(1)} %copy-done.3, bf16[1024,1792]{1,0:T(8,128)(2,1)S(1)} %copy-done.9, bf16[1024,1792]{1,0:T(8,128)(2,1)} %bitcast.4.far_any.far_ref, bf16[3,1024,1024]{2,1,0:T(8,128)(2,1)} %get-tuple-element.32.g_ref, ...), custom_call_target="tpu_custom_call" | custom-call | flops 2147483648 | bytes 4194304 | tf_op jit(solution)/shard_map/pallas_call | solution.py:373
  123.8 9.5 %shard_map.141 = (f32[1024,512]{1,0:T(8,128)}, f32[1024,512]{1,0:T(8,128)S(1)}) custom-call(bf16[1024,1792]{1,0:T(8,128)(2,1)S(1)} %copy-done.4, bf16[1024,1792]{1,0:T(8,128)(2,1)S(1)} %copy-done.9, bf16[1024,1792]{1,0:T(8,128)(2,1)} %bitcast.4.far_any.far_ref, bf16[3,1024,1024]{2,1,0:T(8,128)(2,1)} %get-tuple-element.32.g_ref, ...), custom_call_target="tpu_custom_call" | custom-call | flops 4294967296 | bytes 8388608 | tf_op jit(solution)/shard_map/pallas_call | solution.py:373
  133.2 1.3 copy-done.22
  134.6 16.9 %shard_map.142 = (f32[1024,1024]{1,0:T(8,128)}, f32[1024,1024]{1,0:T(8,128)}) custom-call(bf16[1024,1792]{1,0:T(8,128)(2,1)S(1)} %copy-done.4, bf16[1024,1792]{1,0:T(8,128)(2,1)S(1)} %copy-done.9, bf16[1024,1792]{1,0:T(8,128)(2,1)} %bitcast.4.far_any.far_ref, bf16[3,1024,1024]{2,1,0:T(8,128)(2,1)} %get-tuple-element.32.g_ref, ...), custom_call_target="tpu_custom_call" | custom-call | flops 8589934592 | bytes 16777216 | tf_op jit(solution)/shard_map/pallas_call | solution.py:373
  151.4 6.3 %all-to-all-done.2 = bf16[128,8,1792]{2,1,0:T(8,128)(2,1)} async-done(((bf16[128,8,1792]{2,1,0:T(8,128)(2,1)}), bf16[128,8,1792]{2,1,0:T(8,128)(2,1)}, u32[]{:S(2)}, u32[]{:S(2)}) %all-to-all-start.2) | async-done | bytes 3670048 | tf_op jit(solution)/shard_map/all_to_all | solution.py:32
  157.8 2.2 %copy-done.12 = f32[1024,1024]{1,0:T(8,128)S(1)} copy-done((f32[1024,1024]{1,0:T(8,128)S(1)}, f32[1024,1024]{1,0:T(8,128)}, u32[]{:S(2)}) %copy-start.12) | copy-done | bytes 4194328
  161.2 1.6 copy-done.23
  164.0 22.0 %shard_map.143 = (f32[1024,256]{1,0:T(8,128)}, f32[1024,512]{1,0:T(8,128)}, f32[1024,1024]{1,0:T(8,128)}) custom-call(s32[128,128]{1,0:T(8,128)S(1)} %bitcast.14, bf16[1024,1792]{1,0:T(8,128)(2,1)} %bitcast.9.term_any, f32[1024,256]{1,0:T(8,128)S(1)} %copy-done.27, f32[1024,512]{1,0:T(8,128)S(1)} %copy-done.23, f32[1024,1024]{1,0:T(8,128)S(1)} %copy-done.12, ...), custom_call_target="tpu_custom_call" | custom-call | flops 29360128 | bytes 22020096 | tf_op jit(solution)/shard_map/pallas_call | solution.py:400
  (49 shorter events, 6.5 us)
Async XLA Ops:
  2.2 25.4 %all-to-all-start = ((s32[128,1,128]{2,1,0:T(1,128)}), s32[128,1,128]{2,1,0:T(1,128)S(1)}, u32[]{:S(2)}, u32[]{:S(2)}) async-start(s32[128,1,128]{2,1,0:T(1,128)} %bitcast.20), calls=%async_computation | async-start | bytes 131072 | tf_op jit(solution)/shard_map/all_to_all | solution.py:32
  13.7 1.6 copy-start.10
  15.3 1.2 copy-start.13
  16.6 1.2 copy-start.15
  18.8 1.6 copy-start.20
  24.0 1.8 copy-start
  25.9 1.8 copy-start.6
  27.7 2.0 %copy-start.1 = (bf16[1024,1792]{1,0:T(8,128)(2,1)S(1)}, bf16[1024,1792]{1,0:T(8,128)(2,1)}, u32[]{:S(2)}) copy-start(bf16[1024,1792]{1,0:T(8,128)(2,1)} %copy-done) | copy-start | bytes 11010052
  32.4 1.8 copy-start.5
  34.3 10.2 %copy-start.31 = (s32[1024]{0:T(1024)S(1)}, s32[1024]{0:T(1024)}, u32[]{:S(2)}) copy-start(s32[1024]{0:T(1024)} %param.15) | copy-start | bytes 12292
  34.3 10.2 %copy-start.28 = (s32[4,127]{1,0:T(4,128)S(1)}, s32[4,127]{1,0:T(4,128)}, u32[]{:S(2)}) copy-start(s32[4,127]{1,0:T(4,128)} %neg_ref.1) | copy-start | bytes 6100
  34.3 56.0 %all-to-all-start.1 = ((bf16[128,8,1792]{2,1,0:T(8,128)(2,1)}), bf16[128,8,1792]{2,1,0:T(8,128)(2,1)}, u32[]{:S(2)}, u32[]{:S(2)}) async-start(bf16[128,8,1792]{2,1,0:T(8,128)(2,1)} %bitcast.11), calls=%async_computation.1 | async-start | bytes 7340032 | tf_op jit(solution)/shard_map/all_to_all | solution.py:32
  44.5 2.0 %copy-start.2 = (bf16[1024,1792]{1,0:T(8,128)(2,1)S(1)}, bf16[1024,1792]{1,0:T(8,128)(2,1)}, u32[]{:S(2)}) copy-start(bf16[1024,1792]{1,0:T(8,128)(2,1)} %copy-done) | copy-start | bytes 11010052
  46.5 2.0 %copy-start.7 = (bf16[1024,1792]{1,0:T(8,128)(2,1)S(1)}, bf16[1024,1792]{1,0:T(8,128)(2,1)}, u32[]{:S(2)}) copy-start(bf16[1024,1792]{1,0:T(8,128)(2,1)} %copy-done.6) | copy-start | bytes 11010052
  54.0 1.3 copy-start.29
  90.3 2.0 %copy-start.8 = (bf16[1024,1792]{1,0:T(8,128)(2,1)S(1)}, bf16[1024,1792]{1,0:T(8,128)(2,1)}, u32[]{:S(2)}) copy-start(bf16[1024,1792]{1,0:T(8,128)(2,1)} %copy-done.6) | copy-start | bytes 11010052
  92.3 1.6 copy-start.30
  104.3 1.8 copy-start.17
  106.1 5.7 %copy-start.19 = (bf16[1024,256]{1,0:T(8,128)(2,1)S(1)}, bf16[1024,256]{1,0:T(8,128)(2,1)}, u32[]{:S(2)}) copy-start(bf16[1024,256]{1,0:T(8,128)(2,1)} %raw_ref.3) | copy-start | bytes 1572868
  106.1 51.7 %all-to-all-start.2 = ((bf16[128,8,1792]{2,1,0:T(8,128)(2,1)}), bf16[128,8,1792]{2,1,0:T(8,128)(2,1)}, u32[]{:S(2)}, u32[]{:S(2)}) async-start(bf16[128,8,1792]{2,1,0:T(8,128)(2,1)} %bitcast.12), calls=%async_computation.2 | async-start | bytes 7340032 | tf_op jit(solution)/shard_map/all_to_all | solution.py:32
  111.8 2.0 %copy-start.3 = (bf16[1024,1792]{1,0:T(8,128)(2,1)S(1)}, bf16[1024,1792]{1,0:T(8,128)(2,1)}, u32[]{:S(2)}) copy-start(bf16[1024,1792]{1,0:T(8,128)(2,1)} %copy-done) | copy-start | bytes 11010052
  113.9 2.0 %copy-start.9 = (bf16[1024,1792]{1,0:T(8,128)(2,1)S(1)}, bf16[1024,1792]{1,0:T(8,128)(2,1)}, u32[]{:S(2)}) copy-start(bf16[1024,1792]{1,0:T(8,128)(2,1)} %copy-done.6) | copy-start | bytes 11010052
  115.9 7.8 %copy-start.4 = (bf16[1024,1792]{1,0:T(8,128)(2,1)S(1)}, bf16[1024,1792]{1,0:T(8,128)(2,1)}, u32[]{:S(2)}) copy-start(bf16[1024,1792]{1,0:T(8,128)(2,1)} %copy-done) | copy-start | bytes 11010052
  115.9 7.8 %copy-start.14 = (bf16[1024,512]{1,0:T(8,128)(2,1)S(1)}, bf16[1024,512]{1,0:T(8,128)(2,1)}, u32[]{:S(2)}) copy-start(bf16[1024,512]{1,0:T(8,128)(2,1)} %raw_ref.4) | copy-start | bytes 3145732
  123.1 10.1 %copy-start.26 = (f32[1024,256]{1,0:T(8,128)}, f32[1024,256]{1,0:T(8,128)S(1)}, u32[]{:S(2)}) copy-start(f32[1024,256]{1,0:T(8,128)S(1)} %get-tuple-element.39.dp0) | copy-start | bytes 3145732
  123.7 10.8 %copy-start.21 = (bf16[1024,1024]{1,0:T(8,128)(2,1)S(1)}, bf16[1024,1024]{1,0:T(8,128)(2,1)}, u32[]{:S(2)}) copy-start(bf16[1024,1024]{1,0:T(8,128)(2,1)} %raw_ref.5) | copy-start | bytes 6291460
  133.2 1.3 copy-start.22
  134.6 23.2 %copy-start.11 = (bf16[1024,1024]{1,0:T(8,128)(2,1)S(1)}, bf16[1024,1024]{1,0:T(8,128)(2,1)}, u32[]{:S(2)}) copy-start(bf16[1024,1024]{1,0:T(8,128)(2,1)} %raw2.1) | copy-start | bytes 6291460
  134.6 23.2 %copy-start.25 = (bf16[1024,256]{1,0:T(8,128)(2,1)S(1)}, bf16[1024,256]{1,0:T(8,128)(2,1)}, u32[]{:S(2)}) copy-start(bf16[1024,256]{1,0:T(8,128)(2,1)} %raw0.1) | copy-start | bytes 1572868
  157.8 2.2 %copy-start.12 = (f32[1024,1024]{1,0:T(8,128)S(1)}, f32[1024,1024]{1,0:T(8,128)}, u32[]{:S(2)}) copy-start(f32[1024,1024]{1,0:T(8,128)} %get-tuple-element.41.dp2) | copy-start | bytes 12582916
  160.0 1.2 copy-start.16
  161.2 1.6 copy-start.23
  (3 other events, 3.3 us)
where the time goes:
time: 187 us; the launch traced here: 186 us
  Pallas kernels  78.3 us (42%)
  waiting for transfers between devices  41.2 us (22%)
  local copies, waits for them, and re-layouts  37.7 us (20%)
  starting transfers between devices  27.4 us (15%)
    all_to_all x3, waiting for transfers between devices, exchange(): return lax.all_to_all(values, AXES, split_axis=0, concat_axis=0, tiled=True)  41.2 us
    unnamed x64, local copies, waits for them, and re-layouts  37.7 us
    pallas_call x3, Pallas kernels, local(): pl.pallas_call(functools.partial(near_kernel, k), grid=(lists,), out_shap...  33.5 us
    all_to_all x3, starting transfers between devices, exchange(): return lax.all_to_all(values, AXES, split_axis=0, concat_axis=0, tiled=True)  27.4 us
    pallas_call x1, Pallas kernels, local(): pl.pallas_call(functools.partial(passage_kernel, widths, starts), out_sha...  22 us
    pallas_call x1, Pallas kernels, local(): pl.pallas_call(functools.partial(far_kernel, widths, starts, lists), out_...  10.4 us
    pallas_call x1, Pallas kernels, local(): pl.pallas_call(functools.partial(local_kernel, widths, starts, block_coun...  5.46 us
  transfers between devices with their start and end apart: 3, of which 2 were waited for; matrix products, arithmetic and copies ran while one was open for 0% of the time, Pallas kernels for 22%

commit v1 on v0

--- a/solution.py
+++ b/solution.py
@@ -19,7 +19,7 @@
 
 F32 = jnp.float32
 BF16 = jnp.bfloat16
-ANY = pl.BlockSpec(memory_space=pl.ANY)
+HBM = pl.BlockSpec(memory_space=pltpu.HBM)
 VMEM = pl.BlockSpec(memory_space=pltpu.VMEM)
 SMEM = pl.BlockSpec(memory_space=pltpu.SMEM)
 MIB = 1024 * 1024
@@ -103,13 +103,19 @@
             spos = spos + jnp.sum(jnp.where(row == pos, s, 0.0), axis=0, keepdims=True)
         tot_ref[k : k + 1, :] = tot
         spos_ref[k : k + 1, :] = spos * SHARPNESS
-    far = bias_ref.shape[0]
-    entries = neg_ref.shape[2]
-    peer = lax.broadcasted_iota(jnp.int32, (far, entries), 0) // PROWS
-    local_ids = jnp.broadcast_to(neg_ref[0], (far, entries)) - peer * block_count
-    hit = (local_ids >= 0) & (local_ids < block_count)
-    listed = jnp.max(jnp.where(hit, 1.0, 0.0), axis=1, keepdims=True)
-    bias_ref[...] = jnp.broadcast_to(jnp.where(listed > 0.0, 0.0, OFF), bias_ref.shape)
+    @pl.when(pl.program_id(0) == 0)
+    def _():
+        far = bias_ref.shape[0]
+        lists, entries = neg_ref.shape
+        peer = lax.broadcasted_iota(jnp.int32, (far, entries), 0) // PROWS
+        lane = lax.broadcasted_iota(jnp.int32, bias_ref.shape, 1)
+        bias = jnp.full(bias_ref.shape, OFF, F32)
+        for b in range(lists):
+            local_ids = jnp.broadcast_to(neg_ref[b : b + 1, :], (far, entries)) - peer * block_count
+            hit = (local_ids >= 0) & (local_ids < block_count)
+            listed = jnp.max(jnp.where(hit, 1.0, 0.0), axis=1, keepdims=True)
+            bias = jnp.where((lane == b) & (listed > 0.0), 0.0, bias)
+        bias_ref[...] = bias
 
 
 def far_kernel(
@@ -142,7 +148,7 @@
             tot = tot_ref[k : k + 1, at_q]
             for at in range(0, far, chunk):
                 s = lax.dot_general(far_v[at : at + chunk, span], q, NT, preferred_element_type=F32)
-                bias = bias_ref[at : at + chunk, b * LANES : b * LANES + 1]
+                bias = bias_ref[at : at + chunk, b : b + 1]
                 e = jnp.exp2(s * EXP_SCALE + bias)
                 tot = tot + jnp.sum(e, axis=0, keepdims=True)
                 e_v[at : at + chunk, at_q] = e
@@ -206,15 +212,16 @@
 
 
 def passage_kernel(
-    widths, starts, asked_ref, term_any, dp0, dp1, dp2, raw0, raw1, raw2, inv_ref,
+    widths, starts, place_ref, term_any, dp0, dp1, dp2, raw0, raw1, raw2, inv_ref,
     out0, out1, out2,
-    term_v, acc0, acc1, acc2, rv0, rv1, rv2, in_sems, out_sems,
+    term_v, pick_v, acc0, acc1, acc2, rv0, rv1, rv2, in_sems, out_sems,
 ):
     dps, raws, outs = (dp0, dp1, dp2), (raw0, raw1, raw2), (out0, out1, out2)
     accs, raw_vs = (acc0, acc1, acc2), (rv0, rv1, rv2)
     rows = acc0.shape[0]
-    peers = term_v.shape[0] // PROWS
+    far = term_v.shape[0]
     order = (0, 1, 2)
+    chunk = min(256, rows)
     loads = {}
     for k in order:
         span = pl.ds(starts[k], widths[k])
@@ -225,36 +232,26 @@
         )
         for load in loads[k]:
             load.start()
+    place = place_ref[0:1, :]
+    for at in range(0, rows, chunk):
+        row = lax.broadcasted_iota(jnp.int32, (chunk, far), 0) + at
+        pick_v[at : at + chunk, :] = jnp.where(row == place, 1.0, 0.0).astype(BF16)
     stores = []
-    chunk = rows // 4
     for k in order:
         for load in loads[k]:
             load.wait()
-        acc, raw = accs[k], raw_vs[k]
-        span = pl.ds(starts[k], widths[k])
-
-        def add(pair, carry):
-            both = term_v[pl.ds(pl.multiple_of(pair * 16, 16), 16), span].astype(F32)
-            for half in range(2):
-                ident = jnp.maximum(asked_ref[pair * 2 + half, 0], 0)
-                place = pl.ds(pl.multiple_of(ident * PROWS, PROWS), PROWS)
-                acc[place, :] = acc[place, :] + both[half * 8 : half * 8 + 8]
-            return carry
-
-        lax.fori_loop(0, peers // 2, add, 0)
-        for c in range(4):
-            def finish(step, carry):
-                place = pl.ds(pl.multiple_of(c * chunk + step * 32, 32), 32)
-                inverse = inv_ref[place, 3 + k : 4 + k]
-                unit = raw[place, :].astype(F32) * inverse
-                dp = acc[place, :]
-                dot = jnp.sum(unit * dp, axis=1, keepdims=True)
-                acc[place, :] = (dp - unit * dot) * inverse
-                return carry
-
-            lax.fori_loop(0, chunk // 32, finish, 0)
-            part = pl.ds(c * chunk, chunk)
-            store = pltpu.make_async_copy(acc.at[part, :], outs[k].at[part, :], out_sems.at[k, c])
+        terms = term_v[:, starts[k] : starts[k] + widths[k]]
+        for at in range(0, rows, chunk):
+            here = slice(at, at + chunk)
+            inverse = inv_ref[here, 3 + k : 4 + k]
+            unit = raw_vs[k][here, :].astype(F32) * inverse
+            dp = accs[k][here, :] + jnp.dot(pick_v[here, :], terms, preferred_element_type=F32)
+            dot = jnp.sum(unit * dp, axis=1, keepdims=True)
+            accs[k][here, :] = (dp - unit * dot) * inverse
+            part = pl.ds(at, chunk)
+            store = pltpu.make_async_copy(
+                accs[k].at[part, :], outs[k].at[part, :], out_sems.at[k, at // chunk]
+            )
             store.start()
             stores.append(store)
     for store in stores:
@@ -285,6 +282,7 @@
         out_shape=jax.ShapeDtypeStruct((devices, LANES), jnp.int32),
         in_specs=[VMEM],
         out_specs=VMEM,
+        compiler_params=params(vmem_limit_bytes=62 * MIB),
     )(neg_blocks)
     asked = exchange(wanted[:, None, :]).reshape(devices, LANES)
 
@@ -300,7 +298,7 @@
         ),
         in_specs=[row_block(width) for width in widths + widths],
         out_specs=(row_block(wide), row_block(wide), row_block(LANES)),
-        compiler_params=params(vmem_limit_bytes=24 * MIB),
+        compiler_params=params(vmem_limit_bytes=62 * MIB),
         cost_estimate=cost(rows * wide * 8, rows * wide * 8),
     )(*queries, *passages)
 
@@ -311,7 +309,7 @@
         out_shape=jax.ShapeDtypeStruct((far, wide), BF16),
         in_specs=[SMEM, pl.BlockSpec((rows, wide), lambda i: (0, 0))],
         out_specs=pl.BlockSpec((pairs * 16, wide), lambda i: (i, 0)),
-        compiler_params=params(vmem_limit_bytes=24 * MIB),
+        compiler_params=params(vmem_limit_bytes=62 * MIB),
         cost_estimate=cost(far * wide, far * wide * 4),
     )(asked, p_all)
     fetched = exchange(send.reshape(devices, PROWS, wide)).reshape(far, wide)
@@ -326,18 +324,18 @@
         out_shape=(
             jax.ShapeDtypeStruct((8, rows), F32),
             jax.ShapeDtypeStruct((8, rows), F32),
-            jax.ShapeDtypeStruct((far, lists * LANES), F32),
+            jax.ShapeDtypeStruct((far, LANES), F32),
         ),
         in_specs=[
             whole((rows, wide)),
             pl.BlockSpec((cols, wide), lambda i: (i, 0)),
             pos_block,
-            pl.BlockSpec((1, 1, entries), lambda i: (i, 0, 0)),
+            whole((lists, entries)),
         ],
-        out_specs=(lane_block, lane_block, pl.BlockSpec((far, LANES), lambda i: (0, i))),
-        compiler_params=params(vmem_limit_bytes=32 * MIB),
+        out_specs=(lane_block, lane_block, whole((far, LANES))),
+        compiler_params=params(vmem_limit_bytes=62 * MIB),
         cost_estimate=cost(2 * rows * rows * wide, rows * wide * 4),
-    )(p_all, q_all, local_pos, neg_blocks.reshape(lists, 1, entries))
+    )(p_all, q_all, local_pos, neg_blocks)
 
     terms, far_weights, scales, loss_rows = pl.pallas_call(
         functools.partial(far_kernel, widths, starts, lists),
@@ -347,8 +345,8 @@
             jax.ShapeDtypeStruct((8, rows), F32),
             jax.ShapeDtypeStruct((8, rows), F32),
         ),
-        in_specs=[ANY, ANY, VMEM, VMEM, VMEM],
-        out_specs=(ANY, ANY, VMEM, VMEM),
+        in_specs=[HBM, HBM, VMEM, VMEM, VMEM],
+        out_specs=(HBM, HBM, VMEM, VMEM),
         scratch_shapes=[
             pltpu.VMEM((far, wide), BF16),
             pltpu.VMEM((rows, wide), BF16),
@@ -359,7 +357,7 @@
             pltpu.SemaphoreType.DMA((3,)),
             pltpu.SemaphoreType.DMA((3,)),
         ],
-        compiler_params=params(vmem_limit_bytes=40 * MIB),
+        compiler_params=params(vmem_limit_bytes=62 * MIB),
         cost_estimate=cost(4 * far * rows * wide, 6 * far * wide),
     )(fetched, q_all, bias, totals, positive_scores)
     losses = loss_rows[0] + loss_rows[1] + loss_rows[2]
@@ -391,24 +389,27 @@
                 pl.BlockSpec((cols, width), lambda i: (i, 0)),
                 pl.BlockSpec((rows, width), lambda i: (0, 0)),
             ),
-            compiler_params=params(vmem_limit_bytes=40 * MIB),
+            compiler_params=params(vmem_limit_bytes=62 * MIB),
             cost_estimate=cost(8 * rows * rows * width, 16 * rows * width),
         )(p_all, q_all, fetched, far_weights, queries[k], inverses, scales, local_pos)
         q_grads.append(q_grad)
         dp_parts.append(dp_part)
 
+    offsets = jnp.arange(PROWS, dtype=jnp.int32)
+    asked_ids = asked[:, :1]
+    place = jnp.where(asked_ids >= 0, asked_ids * PROWS + offsets[None, :], -1).reshape(1, far)
     p_grads = pl.pallas_call(
         functools.partial(passage_kernel, widths, starts),
         out_shape=tuple(jax.ShapeDtypeStruct((rows, width), F32) for width in widths),
-        in_specs=[SMEM] + [ANY] * 7 + [VMEM],
-        out_specs=(ANY, ANY, ANY),
-        scratch_shapes=[pltpu.VMEM((far, wide), BF16)]
+        in_specs=[VMEM] + [HBM] * 7 + [VMEM],
+        out_specs=(HBM, HBM, HBM),
+        scratch_shapes=[pltpu.VMEM((far, wide), BF16), pltpu.VMEM((rows, far), BF16)]
         + [pltpu.VMEM((rows, width), F32) for width in widths]
         + [pltpu.VMEM((rows, width), BF16) for width in widths]
         + [pltpu.SemaphoreType.DMA((3, 3)), pltpu.SemaphoreType.DMA((3, 4))],
-        compiler_params=params(vmem_limit_bytes=32 * MIB),
+        compiler_params=params(vmem_limit_bytes=62 * MIB),
         cost_estimate=cost(16 * rows * wide, 12 * rows * wide),
-    )(asked, returned, *dp_parts, *passages, inverses)
+    )(place, returned, *dp_parts, *passages, inverses)
     return (losses, *q_grads, *p_grads)
 
 

time: 187 us -> 164 us (0.88)
  local copies, waits for them, and re-layouts: 37.7 us -> 1.33 us
  Pallas kernels: 78.3 us -> 87.7 us
  waiting for transfers between devices: 41.2 us -> 43.9 us
    unnamed x64 -> x6, local copies, waits for them, and re-layouts: 37.7 us -> 0.64 us
    pallas_call x1, Pallas kernels: 22 us -> 11.4 us  [local(): pl.pallas_call(functools.partial(passage_kernel, widths, starts), out_sha...]
    pallas_call x1, Pallas kernels: 2.54 us -> 9.25 us  [local(): pl.pallas_call(functools.partial(heads_kernel, widths, starts), grid=(8,)...]
    pallas_call x1, Pallas kernels: 10.4 us -> 14.5 us  [local(): pl.pallas_call(functools.partial(far_kernel, widths, starts, lists), out_...]
    pallas_call x1, Pallas kernels: 5.46 us -> 9.13 us  [local(): pl.pallas_call(functools.partial(local_kernel, widths, starts, block_coun...]
    pallas_call x1, Pallas kernels: 2.73 us -> 5.77 us  [local(): pl.pallas_call(functools.partial(gather_kernel, pairs), grid=(devices //...]
    all_to_all x3, waiting for transfers between devices: 41.2 us -> 43.9 us  [exchange(): return lax.all_to_all(values, AXES, split_axis=0, concat_axis=0, tiled=True)]
    pallas_call x3, Pallas kernels: 33.5 us -> 36 us  [local(): pl.pallas_call(functools.partial(near_kernel, k), grid=(lists,), out_shap...]
  transfers between devices with their start and end apart: 3 -> 3, of which waited for: 2 -> 3; matrix products, arithmetic and copies ran while one was open for 0% -> 2% of each run, Pallas kernels for 22% -> 33%
where the time goes in v1:
time: 164 us; the launch traced here: 163 us
  Pallas kernels  87.7 us (53%)
  waiting for transfers between devices  43.9 us (27%)
  starting transfers between devices  26.8 us (16%)
  other arithmetic  2.39 us (1%)
    all_to_all x3, waiting for transfers between devices, exchange(): return lax.all_to_all(values, AXES, split_axis=0, concat_axis=0, tiled=True)  43.9 us
    pallas_call x3, Pallas kernels, local(): pl.pallas_call(functools.partial(near_kernel, k), grid=(lists,), out_shap...  36 us
    all_to_all x3, starting transfers between devices, exchange(): return lax.all_to_all(values, AXES, split_axis=0, concat_axis=0, tiled=True)  26.8 us
    pallas_call x1, Pallas kernels, local(): pl.pallas_call(functools.partial(far_kernel, widths, starts, lists), out_...  14.5 us
    pallas_call x1, Pallas kernels, local(): pl.pallas_call(functools.partial(passage_kernel, widths, starts), out_sha...  11.4 us
    pallas_call x1, Pallas kernels, local(): pl.pallas_call(functools.partial(heads_kernel, widths, starts), grid=(8,)...  9.25 us
    pallas_call x1, Pallas kernels, local(): pl.pallas_call(functools.partial(local_kernel, widths, starts, block_coun...  9.13 us
    pallas_call x1, Pallas kernels, local(): pl.pallas_call(functools.partial(gather_kernel, pairs), grid=(devices //...  5.77 us
  transfers between devices with their start and end apart: 3, of which 3 were waited for; matrix products, arithmetic and copies ran while one was open for 2% of the time, Pallas kernels for 33%

profile of v1, /device:TPU:1, one launch (start us, length us, event | category | flops | bytes accessed | tf_op | source)
XLA Modules:
  0.0 163.0 jit_solution(2715542021413285780)
XLA Ops:
  0.6 1.6 shard_map.135
  2.2 11.5 %all-to-all-start = ((s32[128,1,128]{2,1,0:T(1,128)}), s32[128,1,128]{2,1,0:T(1,128)S(1)}, u32[]{:S(2)}, u32[]{:S(2)}) async-start(s32[128,1,128]{2,1,0:T(1,128)} %bitcast.15), calls=%async_computation | async-start | bytes 131072 | tf_op jit(solution)/shard_map/all_to_all | solution.py:32
  13.7 9.2 %shard_map.136 = (bf16[1024,1792]{1,0:T(8,128)(2,1)}, bf16[1024,1792]{1,0:T(8,128)(2,1)}, f32[1024,128]{1,0:T(8,128)}) custom-call(bf16[1024,256]{1,0:T(8,128)(2,1)} %raw_ref.3, bf16[1024,512]{1,0:T(8,128)(2,1)} %raw_ref.4, bf16[1024,1024]{1,0:T(8,128)(2,1)} %raw_ref.5, bf16[1024,256]{1,0:T(8,128)(2,1)} %raw0.1, bf16[1024,512]{1,0:T(8,128)(2,1)} %raw1.1, ...), custom_call_target="tpu_custom_call" | custom-call | flops 14680064 | bytes 14680064 | tf_op jit(solution)/shard_map/pallas_call | solution.py:291
  23.0 0.5 all-to-all-done
  23.4 0.0 copy-start
  23.4 0.6 copy-done
  24.1 5.8 %shard_map.137 = bf16[1024,1792]{1,0:T(8,128)(2,1)} custom-call(s32[128,128]{1,0:T(8,128)} %bitcast.12, bf16[1024,1792]{1,0:T(8,128)(2,1)} %get-tuple-element.26.p_ref), custom_call_target="tpu_custom_call" | custom-call | flops 1835008 | bytes 7340032 | tf_op jit(solution)/shard_map/pallas_call | solution.py:306
  29.8 0.0 copy-start.2
  29.8 9.7 %all-to-all-start.1 = ((bf16[128,8,1792]{2,1,0:T(8,128)(2,1)}), bf16[128,8,1792]{2,1,0:T(8,128)(2,1)}, u32[]{:S(2)}, u32[]{:S(2)}) async-start(bf16[128,8,1792]{2,1,0:T(8,128)(2,1)} %bitcast.10), calls=%async_computation.1 | async-start | bytes 7340032 | tf_op jit(solution)/shard_map/all_to_all | solution.py:32
  39.6 0.0 copy-done.2
  39.6 0.6 broadcast_subtract_fusion
  40.2 9.1 %shard_map.138 = (f32[8,1024]{1,0:T(8,128)}, f32[8,1024]{1,0:T(8,128)}, f32[1024,128]{1,0:T(8,128)}) custom-call(bf16[1024,1792]{1,0:T(8,128)(2,1)} %get-tuple-element.26.p_ref, bf16[1024,1792]{1,0:T(8,128)(2,1)} %get-tuple-element.27.q_ref.q_any, s32[1,1024]{1,0:T(1,128)} %bitcast.16, s32[4,127]{1,0:T(4,128)} %neg_ref.3), custom_call_target="tpu_custom_call" | custom-call | flops 3758096384 | bytes 7340032 | tf_op jit(solution)/shard_map/pallas_call | solution.py:321
  49.3 36.1 %all-to-all-done.1 = bf16[128,8,1792]{2,1,0:T(8,128)(2,1)} async-done(((bf16[128,8,1792]{2,1,0:T(8,128)(2,1)}), bf16[128,8,1792]{2,1,0:T(8,128)(2,1)}, u32[]{:S(2)}, u32[]{:S(2)}) %all-to-all-start.1) | async-done | bytes 3670048 | tf_op jit(solution)/shard_map/all_to_all | solution.py:32
  85.4 14.5 %shard_map.139 = (bf16[1024,1792]{1,0:T(8,128)(2,1)}, bf16[3,1024,1024]{2,1,0:T(8,128)(2,1)}, f32[8,1024]{1,0:T(8,128)}, f32[8,1024]{1,0:T(8,128)}) custom-call(bf16[1024,1792]{1,0:T(8,128)(2,1)} %bitcast.4.far_any.far_ref, bf16[1024,1792]{1,0:T(8,128)(2,1)} %get-tuple-element.27.q_ref.q_any, f32[1024,128]{1,0:T(8,128)} %get-tuple-element.28.bias_ref, ...), custom_call_target="tpu_custom_call" | custom-call | flops 7516192768 | bytes 11010048 | tf_op jit(solution)/shard_map/pallas_call | solution.py:340
  99.9 0.0 copy-start.1
  99.9 5.6 %all-to-all-start.2 = ((bf16[128,8,1792]{2,1,0:T(8,128)(2,1)}), bf16[128,8,1792]{2,1,0:T(8,128)(2,1)}, u32[]{:S(2)}, u32[]{:S(2)}) async-start(bf16[128,8,1792]{2,1,0:T(8,128)(2,1)} %bitcast.11), calls=%async_computation.2 | async-start | bytes 7340032 | tf_op jit(solution)/shard_map/all_to_all | solution.py:32
  105.5 0.0 copy-done.1
  105.5 0.1 multiply_reduce_fusion
  105.6 0.1 compare_reduce_fusion
  105.7 0.1 add_select_fusion
  105.9 0.7 select_n.15.place_ref
  106.5 7.7 %shard_map.140 = (f32[1024,256]{1,0:T(8,128)}, f32[1024,256]{1,0:T(8,128)}) custom-call(bf16[1024,1792]{1,0:T(8,128)(2,1)} %get-tuple-element.26.p_ref, bf16[1024,1792]{1,0:T(8,128)(2,1)} %get-tuple-element.27.q_ref.q_any, bf16[1024,1792]{1,0:T(8,128)(2,1)} %bitcast.4.far_any.far_ref, bf16[3,1024,1024]{2,1,0:T(8,128)(2,1)} %get-tuple-element.32.g_ref, ...), custom_call_target="tpu_custom_call" | custom-call | flops 2147483648 | bytes 4194304 | tf_op jit(solution)/shard_map/pallas_call | solution.py:371
  114.3 1.5 slice_add_fusion
  115.8 10.6 %shard_map.141 = (f32[1024,512]{1,0:T(8,128)}, f32[1024,512]{1,0:T(8,128)}) custom-call(bf16[1024,1792]{1,0:T(8,128)(2,1)} %get-tuple-element.26.p_ref, bf16[1024,1792]{1,0:T(8,128)(2,1)} %get-tuple-element.27.q_ref.q_any, bf16[1024,1792]{1,0:T(8,128)(2,1)} %bitcast.4.far_any.far_ref, bf16[3,1024,1024]{2,1,0:T(8,128)(2,1)} %get-tuple-element.32.g_ref, ...), custom_call_target="tpu_custom_call" | custom-call | flops 4294967296 | bytes 8388608 | tf_op jit(solution)/shard_map/pallas_call | solution.py:371
  126.3 17.7 %shard_map.142 = (f32[1024,1024]{1,0:T(8,128)}, f32[1024,1024]{1,0:T(8,128)}) custom-call(bf16[1024,1792]{1,0:T(8,128)(2,1)} %get-tuple-element.26.p_ref, bf16[1024,1792]{1,0:T(8,128)(2,1)} %get-tuple-element.27.q_ref.q_any, bf16[1024,1792]{1,0:T(8,128)(2,1)} %bitcast.4.far_any.far_ref, bf16[3,1024,1024]{2,1,0:T(8,128)(2,1)} %get-tuple-element.32.g_ref, ...), custom_call_target="tpu_custom_call" | custom-call | flops 8589934592 | bytes 16777216 | tf_op jit(solution)/shard_map/pallas_call | solution.py:371
  144.1 7.4 %all-to-all-done.2 = bf16[128,8,1792]{2,1,0:T(8,128)(2,1)} async-done(((bf16[128,8,1792]{2,1,0:T(8,128)(2,1)}), bf16[128,8,1792]{2,1,0:T(8,128)(2,1)}, u32[]{:S(2)}, u32[]{:S(2)}) %all-to-all-start.2) | async-done | bytes 3670048 | tf_op jit(solution)/shard_map/all_to_all | solution.py:32
  151.4 11.4 %shard_map.143 = (f32[1024,256]{1,0:T(8,128)}, f32[1024,512]{1,0:T(8,128)}, f32[1024,1024]{1,0:T(8,128)}) custom-call(s32[1,1024]{1,0:T(1,128)} %select_n.15.place_ref, bf16[1024,1792]{1,0:T(8,128)(2,1)} %bitcast.8.term_any, f32[1024,256]{1,0:T(8,128)} %get-tuple-element.39.dp0, f32[1024,512]{1,0:T(8,128)} %get-tuple-element.40.dp1, ...), custom_call_target="tpu_custom_call" | custom-call | flops 29360128 | bytes 22020096 | tf_op jit(solution)/shard_map/pallas_call | solution.py:401
Async XLA Ops:
  2.2 21.2 %all-to-all-start = ((s32[128,1,128]{2,1,0:T(1,128)}), s32[128,1,128]{2,1,0:T(1,128)S(1)}, u32[]{:S(2)}, u32[]{:S(2)}) async-start(s32[128,1,128]{2,1,0:T(1,128)} %bitcast.15), calls=%async_computation | async-start | bytes 131072 | tf_op jit(solution)/shard_map/all_to_all | solution.py:32
  23.4 0.6 copy-start
  29.8 9.7 %copy-start.2 = (s32[1024]{0:T(1024)S(1)}, s32[1024]{0:T(1024)}, u32[]{:S(2)}) copy-start(s32[1024]{0:T(1024)} %param.15) | copy-start | bytes 12292
  29.8 55.5 %all-to-all-start.1 = ((bf16[128,8,1792]{2,1,0:T(8,128)(2,1)}), bf16[128,8,1792]{2,1,0:T(8,128)(2,1)}, u32[]{:S(2)}, u32[]{:S(2)}) async-start(bf16[128,8,1792]{2,1,0:T(8,128)(2,1)} %bitcast.10), calls=%async_computation.1 | async-start | bytes 7340032 | tf_op jit(solution)/shard_map/all_to_all | solution.py:32
  99.9 5.6 %copy-start.1 = (s32[128,1,128]{2,1,0:T(1,128)S(1)}, s32[128,1,128]{2,1,0:T(1,128)}, u32[]{:S(2)}) copy-start(s32[128,1,128]{2,1,0:T(1,128)} %copy-done) | copy-start | bytes 196612
  99.9 51.5 %all-to-all-start.2 = ((bf16[128,8,1792]{2,1,0:T(8,128)(2,1)}), bf16[128,8,1792]{2,1,0:T(8,128)(2,1)}, u32[]{:S(2)}, u32[]{:S(2)}) async-start(bf16[128,8,1792]{2,1,0:T(8,128)(2,1)} %bitcast.11), calls=%async_computation.2 | async-start | bytes 7340032 | tf_op jit(solution)/shard_map/all_to_all | solution.py:32

commit v2 on v1

v2 whole, which is shorter than its diff:
```python
import functools
import math

import jax
import jax.numpy as jnp
from jax import lax
from jax.experimental import pallas as pl
from jax.experimental.pallas import tpu as pltpu
from jax.sharding import PartitionSpec as P

PROWS = 8
LANES = 128
AXES = ("dp", "group")

EPSILON = 1e-06
SHARPNESS = 20.0
EXP_SCALE = SHARPNESS * math.log2(math.e)
OFF = -1e30

F32 = jnp.float32
BF16 = jnp.bfloat16
HBM = pl.BlockSpec(memory_space=pltpu.HBM)
VMEM = pl.BlockSpec(memory_space=pltpu.VMEM)
SMEM = pl.BlockSpec(memory_space=pltpu.SMEM)
MIB = 1024 * 1024
NT = (((1,), (1,)), ((), ()))
TN = (((0,), (0,)), ((), ()))
NN = (((1,), (0,)), ((), ()))


def exchange(values):
    return lax.all_to_all(values, AXES, split_axis=0, concat_axis=0, tiled=True)


def cost(flops, moved):
    return pl.CostEstimate(flops=int(flops), bytes_accessed=int(moved), transcendentals=0)


def columns_of(widths):
    starts = {}
    at = 0
    for index in sorted(range(len(widths)), key=lambda i: -widths[i]):
        starts[index] = at
        at += widths[index]
    return [starts[i] for i in range(len(widths))]


def wanted_kernel(block_count, neg_ref, out_ref):
    peers = out_ref.shape[0]
    lists, entries = neg_ref.shape
    peer = lax.broadcasted_iota(jnp.int32, (peers, entries), 0)
    best = jnp.full((peers, 1), -1, jnp.int32)
    for row in range(lists):
        ids = jnp.broadcast_to(neg_ref[row : row + 1, :], (peers, entries))
        local_ids = ids - peer * block_count
        hit = (local_ids >= 0) & (local_ids < block_count)
        best = jnp.maximum(best, jnp.max(jnp.where(hit, local_ids, -1), axis=1, keepdims=True))
    out_ref[...] = jnp.broadcast_to(best, out_ref.shape)


def heads_kernel(widths, starts, raw0, raw1, raw2, after_ref, out_ref, inv_ref):
    del after_ref
    lane = lax.broadcasted_iota(jnp.int32, inv_ref.shape, 1)
    packed = jnp.zeros(inv_ref.shape, F32)
    for k, raw in enumerate((raw0, raw1, raw2)):
        values = raw[...].astype(F32)
        inverse = lax.rsqrt(jnp.sum(values * values, axis=1, keepdims=True) + EPSILON)
        out_ref[:, starts[k] : starts[k] + widths[k]] = (values * inverse).astype(BF16)
        packed = jnp.where(lane == k, inverse, packed)
    inv_ref[...] = packed


def gather_kernel(asked_ref, p_ref, out_hbm, out_v, sems):
    pairs = out_v.shape[0] // 16
    parts = min(8, pairs)
    each = pairs // parts

    def block(peer):
        ident = jnp.maximum(asked_ref[peer, 0], 0)
        start = pl.multiple_of((ident // 2) * 16, 16)
        both = p_ref[pl.ds(start, 16), :].astype(F32)
        return jnp.where(ident % 2 == 0, both[:8], both[8:])

    stores = []
    for part in range(parts):
        for pair in range(part * each, (part + 1) * each):
            rows = jnp.concatenate([block(pair * 2), block(pair * 2 + 1)], axis=0)
            out_v[pair * 16 : pair * 16 + 16, :] = rows.astype(BF16)
        here = pl.ds(part * each * 16, each * 16)
        store = pltpu.make_async_copy(out_v.at[here, :], out_hbm.at[here, :], sems.at[part])
        store.start()
        stores.append(store)
    for store in stores:
        store.wait()


def local_kernel(
    widths, starts, block_count, p_ref, q_ref, pos_ref, neg_ref,
    tot_ref, spos_ref, bias_ref, e_ref,
):
    rows = p_ref.shape[0]
    cols = pos_ref.shape[1]
    chunk = min(256, rows)
    pos = pos_ref[0:1, :]
    for k in range(3):
        span = slice(starts[k], starts[k] + widths[k])
        q = q_ref[:, span]
        tot = jnp.zeros((1, cols), F32)
        spos = jnp.zeros((1, cols), F32)
        for at in range(0, rows, chunk):
            s = lax.dot_general(p_ref[at : at + chunk, span], q, NT, preferred_element_type=F32)
            row = lax.broadcasted_iota(jnp.int32, (chunk, cols), 0) + at
            e = jnp.exp2(s * EXP_SCALE)
            e_ref[k, at : at + chunk, :] = e.astype(BF16)
            tot = tot + jnp.sum(e, axis=0, keepdims=True)
            spos = spos + jnp.sum(jnp.where(row == pos, s, 0.0), axis=0, keepdims=True)
        tot_ref[k : k + 1, :] = tot
        spos_ref[k : k + 1, :] = spos * SHARPNESS
    @pl.when(pl.program_id(0) == 0)
    def _():
        far = bias_ref.shape[0]
        lists, entries = neg_ref.shape
        peer = lax.broadcasted_iota(jnp.int32, (far, entries), 0) // PROWS
        lane = lax.broadcasted_iota(jnp.int32, bias_ref.shape, 1)
        bias = jnp.full(bias_ref.shape, OFF, F32)
        for b in range(lists):
            local_ids = jnp.broadcast_to(neg_ref[b : b + 1, :], (far, entries)) - peer * block_count
            hit = (local_ids >= 0) & (local_ids < block_count)
            listed = jnp.max(jnp.where(hit, 1.0, 0.0), axis=1, keepdims=True)
            bias = jnp.where((lane == b) & (listed > 0.0), 0.0, bias)
        bias_ref[...] = bias


def far_kernel(
    widths, starts, lists, far_hbm, q_hbm, bias_ref, tot_ref, spos_ref,
    term_hbm, scale_ref, loss_ref,
    far_ref, q_ref, g_ref, e_v, term_v, in_sems, out_sems,
):
    far, rows = g_ref.shape
    cols = rows // lists
    chunk = min(256, far)
    order = (0, 1, 2)
    loads = {}
    for k in order:
        span = pl.ds(starts[k], widths[k])
        loads[k] = (
            pltpu.make_async_copy(far_hbm.at[:, span], far_ref.at[:, span], in_sems.at[k, 0]),
            pltpu.make_async_copy(q_hbm.at[:, span], q_ref.at[:, span], in_sems.at[k, 1]),
        )
        for load in loads[k]:
            load.start()
    stores = []
    step = 256
    for k in order:
        span = slice(starts[k], starts[k] + widths[k])
        for load in loads[k]:
            load.wait()
        for b in range(lists):
            at_q = slice(b * cols, (b + 1) * cols)
            q = q_ref[at_q, span]
            tot = tot_ref[k : k + 1, at_q]
            for at in range(0, far, chunk):
                s = lax.dot_general(far_ref[at : at + chunk, span], q, NT, preferred_element_type=F32)
                bias = bias_ref[at : at + chunk, b : b + 1]
                e = jnp.exp2(s * EXP_SCALE + bias)
                tot = tot + jnp.sum(e, axis=0, keepdims=True)
                e_v[at : at + chunk, at_q] = e
            scale = SHARPNESS / tot
            scale_ref[k : k + 1, at_q] = scale
            loss_ref[k : k + 1, at_q] = jnp.log(tot) - spos_ref[k : k + 1, at_q]
            for at in range(0, far, chunk):
                g_ref[at : at + chunk, at_q] = (e_v[at : at + chunk, at_q] * scale).astype(BF16)
        for at in range(starts[k], starts[k] + widths[k], step):
            here = slice(at, at + step)
            for row in range(0, far, chunk):
                part = jnp.dot(g_ref[row : row + chunk, :], q_ref[:, here], preferred_element_type=F32)
                term_v[row : row + chunk, here] = part.astype(BF16)
            here = pl.ds(at, step)
            store = pltpu.make_async_copy(
                term_v.at[:, here], term_hbm.at[:, here], out_sems.at[at // step]
            )
            store.start()
            stores.append(store)
    for store in stores:
        store.wait()


def raw_gradient(raw, inverse, grad):
    unit = raw.astype(F32) * inverse
    return (grad - unit * jnp.sum(unit * grad, axis=1, keepdims=True)) * inverse


def near_kernel(
    k, lists, p_ref, q_ref, far_ref, e_ref, raw_ref, inv_ref, scale_ref, bias_ref, pos_ref,
    p_raw_ref, p_inv_ref, out_ref, part_ref, dp_v,
):
    rows = p_ref.shape[0]
    far = far_ref.shape[0]
    cols = q_ref.shape[0]
    q = q_ref[...]
    pos = pos_ref[0:1, :]
    scale = scale_ref[k : k + 1, :]
    chunk = min(256, rows, far)
    step = pl.program_id(0)
    lane = lax.broadcasted_iota(jnp.int32, (chunk, LANES), 1)
    parts = []
    for at in range(0, far, chunk):
        s = lax.dot_general(far_ref[at : at + chunk, :], q, NT, preferred_element_type=F32)
        bias = jnp.sum(jnp.where(lane == step, bias_ref[at : at + chunk, :], 0.0), axis=1, keepdims=True)
        parts.append((jnp.exp2(s * EXP_SCALE + bias) * scale).astype(BF16))
    dq = lax.dot_general(
        jnp.concatenate(parts, axis=0), far_ref[...], TN, preferred_element_type=F32
    )
    parts = []
    for at in range(0, rows, chunk):
        row = lax.broadcasted_iota(jnp.int32, (chunk, cols), 0) + at
        g = e_ref[0, at : at + chunk, :].astype(F32) * scale
        parts.append((g - jnp.where(row == pos, SHARPNESS, 0.0)).astype(BF16))
    weights = jnp.concatenate(parts, axis=0)
    dq = dq + lax.dot_general(weights, p_ref[...], TN, preferred_element_type=F32)
    dp = jnp.dot(weights, q, preferred_element_type=F32)

    @pl.when(step == 0)
    def _():
        dp_v[...] = dp

    @pl.when(step > 0)
    def _():
        dp_v[...] += dp

    out_ref[...] = raw_gradient(raw_ref[...], inv_ref[:, k : k + 1], dq)

    @pl.when(step == lists - 1)
    def _():
        for at in range(0, rows, chunk):
            here = slice(at, at + chunk)
            part = raw_gradient(p_raw_ref[here, :], p_inv_ref[here, k : k + 1], dp_v[here, :])
            part_ref[here, :] = part.astype(BF16)


def passage_kernel(
    widths, starts, place_ref, term_hbm, part0, part1, part2, raw0, raw1, raw2, inv_ref,
    out0, out1, out2,
    term_v, pick_v, dv0, dv1, dv2, rv0, rv1, rv2, ov0, ov1, ov2, in_sems, out_sems,
):
    parts, raws, outs = (part0, part1, part2), (raw0, raw1, raw2), (out0, out1, out2)
    part_vs, raw_vs, out_vs = (dv0, dv1, dv2), (rv0, rv1, rv2), (ov0, ov1, ov2)
    rows = ov0.shape[0]
    far = term_v.shape[0]
    order = (0, 1, 2)
    chunk = min(256, rows)
    loads = {}
    for k in order:
        span = pl.ds(starts[k], widths[k])
        loads[k] = (
            pltpu.make_async_copy(term_hbm.at[:, span], term_v.at[:, span], in_sems.at[k, 0]),
            pltpu.make_async_copy(parts[k], part_vs[k], in_sems.at[k, 1]),
            pltpu.make_async_copy(raws[k], raw_vs[k], in_sems.at[k, 2]),
        )
        for load in loads[k]:
            load.start()
    place = place_ref[0:1, :]
    for at in range(0, rows, chunk):
        row = lax.broadcasted_iota(jnp.int32, (chunk, far), 0) + at
        pick_v[at : at + chunk, :] = jnp.where(row == place, 1.0, 0.0).astype(BF16)
    stores = []
    for k in order:
        for load in loads[k]:
            load.wait()
        terms = term_v[:, starts[k] : starts[k] + widths[k]]
        for at in range(0, rows, chunk):
            here = slice(at, at + chunk)
            inverse = inv_ref[here, k : k + 1]
            added = jnp.dot(pick_v[here, :], terms, preferred_element_type=F32)
            added = raw_gradient(raw_vs[k][here, :], inverse, added)
            out_vs[k][here, :] = part_vs[k][here, :].astype(F32) + added
            part = pl.ds(at, chunk)
            store = pltpu.make_async_copy(
                out_vs[k].at[part, :], outs[k].at[part, :], out_sems.at[k, at // chunk]
            )
            store.start()
            stores.append(store)
    for store in stores:
        store.wait()


def local(
    query_first, query_second, query_third,
    passage_first, passage_second, passage_third,
    neg_blocks, positives,
):
    devices = lax.axis_size(AXES)
    own = lax.axis_index(AXES)
    queries = (query_first, query_second, query_third)
    passages = (passage_first, passage_second, passage_third)
    widths = [values.shape[1] for values in queries]
    starts = columns_of(widths)
    wide = sum(widths)
    rows = query_first.shape[0]
    block_count = rows // PROWS
    lists, entries = neg_blocks.shape
    far = devices * PROWS
    cols = rows // lists
    params = pltpu.CompilerParams(vmem_limit_bytes=62 * MIB)
    shape = jax.ShapeDtypeStruct

    wanted = pl.pallas_call(
        functools.partial(wanted_kernel, block_count),
        out_shape=jax.ShapeDtypeStruct((devices, LANES), jnp.int32),
        in_specs=[VMEM],
        out_specs=VMEM,
        compiler_params=params,
    )(neg_blocks)
    asked = exchange(wanted[:, None, :]).reshape(devices, LANES)

    step = rows // 4
    row_block = lambda width: pl.BlockSpec((step, width), lambda i: (i, 0))

    def heads(values, after):
        return pl.pallas_call(
            functools.partial(heads_kernel, widths, starts),
            grid=(4,),
            out_shape=(shape((rows, wide), BF16), shape((rows, LANES), F32)),
            in_specs=[row_block(width) for width in widths] + [HBM],
            out_specs=(row_block(wide), row_block(LANES)),
            compiler_params=params,
            cost_estimate=cost(rows * wide * 4, rows * wide * 4),
        )(*values, after)

    p_all, p_inverses = heads(passages, wanted)

    send = pl.pallas_call(
        gather_kernel,
        out_shape=shape((far, wide), BF16),
        in_specs=[SMEM, VMEM],
        out_specs=HBM,
        scratch_shapes=[pltpu.VMEM((far, wide), BF16), pltpu.SemaphoreType.DMA((8,))],
        compiler_params=params,
        cost_estimate=cost(far * wide, far * wide * 4),
    )(asked, p_all)
    fetched = exchange(send.reshape(devices, PROWS, wide)).reshape(far, wide)

    q_all, q_inverses = heads(queries, send)
    local_pos = (positives - own * rows).reshape(1, rows)
    whole = lambda dims: pl.BlockSpec(dims, lambda i: (0,) * len(dims))
    pos_block = pl.BlockSpec((1, cols), lambda i: (0, i))
    lane_block = pl.BlockSpec((8, cols), lambda i: (0, i))
    totals, positive_scores, bias, local_exps = pl.pallas_call(
        functools.partial(local_kernel, widths, starts, block_count),
        grid=(lists,),
        out_shape=(
            shape((8, rows), F32),
            shape((8, rows), F32),
            shape((far, LANES), F32),
            shape((3, rows, rows), BF16),
        ),
        in_specs=[
            whole((rows, wide)),
            pl.BlockSpec((cols, wide), lambda i: (i, 0)),
            pos_block,
            whole((lists, entries)),
        ],
        out_specs=(
            lane_block,
            lane_block,
            whole((far, LANES)),
            pl.BlockSpec((3, rows, cols), lambda i: (0, 0, i)),
        ),
        compiler_params=params,
        cost_estimate=cost(2 * rows * rows * wide, rows * wide * 4),
    )(p_all, q_all, local_pos, neg_blocks)

    terms, scales, loss_rows = pl.pallas_call(
        functools.partial(far_kernel, widths, starts, lists),
        out_shape=(shape((far, wide), BF16), shape((8, rows), F32), shape((8, rows), F32)),
        in_specs=[HBM, HBM, VMEM, VMEM, VMEM],
        out_specs=(HBM, VMEM, VMEM),
        scratch_shapes=[
            pltpu.VMEM((far, wide), BF16),
            pltpu.VMEM((rows, wide), BF16),
            pltpu.VMEM((far, rows), BF16),
            pltpu.VMEM((far, rows), F32),
            pltpu.VMEM((far, wide), BF16),
            pltpu.SemaphoreType.DMA((3, 2)),
            pltpu.SemaphoreType.DMA((wide // 256,)),
        ],
        compiler_params=params,
        cost_estimate=cost(4 * far * rows * wide, 6 * far * wide),
    )(fetched, q_all, bias, totals, positive_scores)
    losses = loss_rows[0] + loss_rows[1] + loss_rows[2]
    returned = exchange(terms.reshape(devices, PROWS, wide)).reshape(far, wide)

    q_grads = []
    p_parts = []
    for k in range(3):
        width = widths[k]
        place = starts[k] // width
        q_grad, p_part = pl.pallas_call(
            functools.partial(near_kernel, k, lists),
            grid=(lists,),
            out_shape=(shape((rows, width), F32), shape((rows, width), BF16)),
            in_specs=[
                pl.BlockSpec((rows, width), lambda i, place=place: (0, place)),
                pl.BlockSpec((cols, width), lambda i, place=place: (i, place)),
                pl.BlockSpec((far, width), lambda i, place=place: (0, place)),
                pl.BlockSpec((1, rows, cols), lambda i, k=k: (k, 0, i)),
                pl.BlockSpec((cols, width), lambda i: (i, 0)),
                pl.BlockSpec((cols, LANES), lambda i: (i, 0)),
                lane_block,
                whole((far, LANES)),
                pos_block,
                whole((rows, width)),
                whole((rows, LANES)),
            ],
            out_specs=(pl.BlockSpec((cols, width), lambda i: (i, 0)), whole((rows, width))),
            scratch_shapes=[pltpu.VMEM((rows, width), F32)],
            compiler_params=params,
            cost_estimate=cost(8 * rows * rows * width, 16 * rows * width),
        )(
            p_all, q_all, fetched, local_exps, queries[k], q_inverses, scales, bias, local_pos,
            passages[k], p_inverses,
        )
        q_grads.append(q_grad)
        p_parts.append(p_part)

    offsets = jnp.arange(PROWS, dtype=jnp.int32)
    asked_ids = asked[:, :1]
    place = jnp.where(asked_ids >= 0, asked_ids * PROWS + offsets[None, :], -1).reshape(1, far)
    p_grads = pl.pallas_call(
        functools.partial(passage_kernel, widths, starts),
        out_shape=tuple(shape((rows, width), F32) for width in widths),
        in_specs=[VMEM] + [HBM] * 7 + [VMEM],
        out_specs=(HBM, HBM, HBM),
        scratch_shapes=[pltpu.VMEM((far, wide), BF16), pltpu.VMEM((rows, far), BF16)]
        + [pltpu.VMEM((rows, width), BF16) for width in widths]
        + [pltpu.VMEM((rows, width), BF16) for width in widths]
        + [pltpu.VMEM((rows, width), F32) for width in widths]
        + [pltpu.SemaphoreType.DMA((3, 3)), pltpu.SemaphoreType.DMA((3, 4))],
        compiler_params=params,
        cost_estimate=cost(16 * rows * wide, 12 * rows * wide),
    )(place, returned, *p_parts, *passages, p_inverses)
    return (losses, *q_grads, *p_grads)


def solution(mesh):
    rows = P(AXES, None)
    return jax.shard_map(
        local,
        mesh=mesh,
        in_specs=(rows,) * 7 + (P(AXES),),
        out_specs=(P(AXES),) + (rows,) * 6,
        check_vma=False,
    )
```

time: 164 us -> 155 us (0.945)
  waiting for transfers between devices: 43.9 us -> 37.9 us
  starting transfers between devices: 26.8 us -> 22.7 us
    all_to_all x3, waiting for transfers between devices: 43.9 us -> 37.9 us  [exchange(): return lax.all_to_all(values, AXES, split_axis=0, concat_axis=0, tiled=True)]
    all_to_all x3, starting transfers between devices: 26.8 us -> 22.7 us  [exchange(): return lax.all_to_all(values, AXES, split_axis=0, concat_axis=0, tiled=True)]
    pallas_call x5 -> x6, Pallas kernels: 51.1 us -> 54.1 us  [the longest x3 39.8 us: local(): pl.pallas_call(functools.partial(near_kernel, k, lists), grid=(lists,), o...]
    pallas_call x1, Pallas kernels: 14.5 us -> 12.4 us  [local(): pl.pallas_call(functools.partial(far_kernel, widths, starts, lists), out_...]
  transfers between devices with their start and end apart: 3 -> 3, of which waited for: 3 -> 3; matrix products, arithmetic and copies ran while one was open for 2% -> 2% of each run, Pallas kernels for 33% -> 39%
where the time goes in v2:
time: 155 us; the launch traced here: 154 us
  Pallas kernels  88.8 us (57%)
  waiting for transfers between devices  37.9 us (24%)
  starting transfers between devices  22.7 us (15%)
  other arithmetic  2.39 us (2%)
    pallas_call x3, Pallas kernels, local(): pl.pallas_call(functools.partial(near_kernel, k, lists), grid=(lists,), o...  39.8 us
    all_to_all x3, waiting for transfers between devices, exchange(): return lax.all_to_all(values, AXES, split_axis=0, concat_axis=0, tiled=True)  37.9 us
    all_to_all x3, starting transfers between devices, exchange(): return lax.all_to_all(values, AXES, split_axis=0, concat_axis=0, tiled=True)  22.7 us
    pallas_call x1, Pallas kernels, local(): pl.pallas_call(functools.partial(far_kernel, widths, starts, lists), out_...  12.4 us
    pallas_call x1, Pallas kernels, local(): pl.pallas_call(functools.partial(passage_kernel, widths, starts), out_sha...  10.4 us
    pallas_call x1, Pallas kernels, local(): pl.pallas_call(functools.partial(local_kernel, widths, starts, block_coun...  10.3 us
    pallas_call x2, Pallas kernels, heads(): pl.pallas_call(functools.partial(heads_kernel, widths, starts), grid=(4,)...  10.3 us
    pallas_call x1, Pallas kernels, local(): pl.pallas_call(gather_kernel, out_shape=shape((far, wide), BF16), in_spec...  4.06 us
  transfers between devices with their start and end apart: 3, of which 3 were waited for; matrix products, arithmetic and copies ran while one was open for 2% of the time, Pallas kernels for 39%

profile of v2, /device:TPU:1, one launch (start us, length us, event | category | flops | bytes accessed | tf_op | source)
XLA Modules:
  0.0 154.1 jit_solution(15470979918099585740)
XLA Ops:
  0.6 1.6 %shard_map.135.after_ref = s32[128,128]{1,0:T(8,128)} custom-call(s32[4,127]{1,0:T(4,128)} %neg_ref.3), custom_call_target="tpu_custom_call" | custom-call | tf_op jit(solution)/shard_map/pallas_call | solution.py:307
  2.2 11.5 %all-to-all-start = ((s32[128,1,128]{2,1,0:T(1,128)}), s32[128,1,128]{2,1,0:T(1,128)S(1)}, u32[]{:S(2)}, u32[]{:S(2)}) async-start(s32[128,1,128]{2,1,0:T(1,128)} %bitcast.15), calls=%async_computation | async-start | bytes 131072 | tf_op jit(solution)/shard_map/all_to_all | solution.py:32
  13.7 5.1 %shard_map.136 = (bf16[1024,1792]{1,0:T(8,128)(2,1)}, f32[1024,128]{1,0:T(8,128)}) custom-call(bf16[1024,256]{1,0:T(8,128)(2,1)} %raw0.5, bf16[1024,512]{1,0:T(8,128)(2,1)} %raw1.5, bf16[1024,1024]{1,0:T(8,128)(2,1)} %raw2.5, s32[128,128]{1,0:T(8,128)} %shard_map.135.after_ref), custom_call_target="tpu_custom_call" | custom-call | flops 7340032 | bytes 7340032 | tf_op jit(solution)/shard_map/pallas_call | solution.py:320
  18.8 4.6 %all-to-all-done = s32[128,1,128]{2,1,0:T(1,128)S(1)} async-done(((s32[128,1,128]{2,1,0:T(1,128)}), s32[128,1,128]{2,1,0:T(1,128)S(1)}, u32[]{:S(2)}, u32[]{:S(2)}) %all-to-all-start) | async-done | bytes 65568 | tf_op jit(solution)/shard_map/all_to_all | solution.py:32
  23.4 0.0 copy-start
  23.4 0.6 copy-done
  24.1 4.1 %shard_map.137.after_ref = bf16[1024,1792]{1,0:T(8,128)(2,1)} custom-call(s32[128,128]{1,0:T(8,128)} %bitcast.12, bf16[1024,1792]{1,0:T(8,128)(2,1)} %get-tuple-element.27.p_ref), custom_call_target="tpu_custom_call" | custom-call | flops 1835008 | bytes 7340032 | tf_op jit(solution)/shard_map/pallas_call | solution.py:332
  28.1 0.0 copy-start.2
  28.2 5.6 %all-to-all-start.1 = ((bf16[128,8,1792]{2,1,0:T(8,128)(2,1)}), bf16[128,8,1792]{2,1,0:T(8,128)(2,1)}, u32[]{:S(2)}, u32[]{:S(2)}) async-start(bf16[128,8,1792]{2,1,0:T(8,128)(2,1)} %bitcast.10), calls=%async_computation.1 | async-start | bytes 7340032 | tf_op jit(solution)/shard_map/all_to_all | solution.py:32
  33.7 0.0 copy-done.2
  33.8 0.6 broadcast_subtract_fusion
  34.3 5.2 %shard_map.138 = (bf16[1024,1792]{1,0:T(8,128)(2,1)}, f32[1024,128]{1,0:T(8,128)}) custom-call(bf16[1024,256]{1,0:T(8,128)(2,1)} %raw_ref.3, bf16[1024,512]{1,0:T(8,128)(2,1)} %raw_ref.4, bf16[1024,1024]{1,0:T(8,128)(2,1)} %raw_ref.5, bf16[1024,1792]{1,0:T(8,128)(2,1)} %shard_map.137.after_ref), custom_call_target="tpu_custom_call" | custom-call | flops 7340032 | bytes 7340032 | tf_op jit(solution)/shard_map/pallas_call | solution.py:320
  39.5 10.3 %shard_map.139 = (f32[8,1024]{1,0:T(8,128)}, f32[8,1024]{1,0:T(8,128)}, f32[1024,128]{1,0:T(8,128)}, bf16[3,1024,1024]{2,1,0:T(8,128)(2,1)}) custom-call(bf16[1024,1792]{1,0:T(8,128)(2,1)} %get-tuple-element.27.p_ref, bf16[1024,1792]{1,0:T(8,128)(2,1)} %get-tuple-element.28.q_ref.q_hbm, s32[1,1024]{1,0:T(1,128)} %bitcast.16, s32[4,127]{1,0:T(4,128)} %neg_ref.3), custom_call_target="tpu_custom_call" | custom-call | flops 3758096384 | bytes 7340032 | tf_op jit(solution)/shard_map/pallas_call | solution.py:348
  49.8 29.8 %all-to-all-done.1 = bf16[128,8,1792]{2,1,0:T(8,128)(2,1)} async-done(((bf16[128,8,1792]{2,1,0:T(8,128)(2,1)}), bf16[128,8,1792]{2,1,0:T(8,128)(2,1)}, u32[]{:S(2)}, u32[]{:S(2)}) %all-to-all-start.1) | async-done | bytes 3670048 | tf_op jit(solution)/shard_map/all_to_all | solution.py:32
  79.5 12.4 %shard_map.140 = (bf16[1024,1792]{1,0:T(8,128)(2,1)}, f32[8,1024]{1,0:T(8,128)}, f32[8,1024]{1,0:T(8,128)}) custom-call(bf16[1024,1792]{1,0:T(8,128)(2,1)} %bitcast.4.far_hbm.far_ref, bf16[1024,1792]{1,0:T(8,128)(2,1)} %get-tuple-element.28.q_ref.q_hbm, f32[1024,128]{1,0:T(8,128)} %get-tuple-element.29.bias_ref, f32[8,1024]{1,0:T(8,128)} %get-tuple-element.30.tot_ref, ...), custom_call_target="tpu_custom_call" | custom-call | flops 7516192768 | bytes 11010048 | tf_op jit(solution)/shard_map/pallas_call | solution.py:373
  92.0 0.0 copy-start.1
  92.0 5.6 %all-to-all-start.2 = ((bf16[128,8,1792]{2,1,0:T(8,128)(2,1)}), bf16[128,8,1792]{2,1,0:T(8,128)(2,1)}, u32[]{:S(2)}, u32[]{:S(2)}) async-start(bf16[128,8,1792]{2,1,0:T(8,128)(2,1)} %bitcast.11), calls=%async_computation.2 | async-start | bytes 7340032 | tf_op jit(solution)/shard_map/all_to_all | solution.py:32
  97.6 0.0 copy-done.1
  97.6 0.1 multiply_reduce_fusion
  97.7 0.1 compare_reduce_fusion
  97.8 0.1 add_select_fusion
  97.9 0.7 select_n.15.place_ref
  98.6 8.6 %shard_map.141 = (f32[1024,256]{1,0:T(8,128)}, bf16[1024,256]{1,0:T(8,128)(2,1)}) custom-call(bf16[1024,1792]{1,0:T(8,128)(2,1)} %get-tuple-element.27.p_ref, bf16[1024,1792]{1,0:T(8,128)(2,1)} %get-tuple-element.28.q_ref.q_hbm, bf16[1024,1792]{1,0:T(8,128)(2,1)} %bitcast.4.far_hbm.far_ref, bf16[3,1024,1024]{2,1,0:T(8,128)(2,1)} %get-tuple-element.33.e_ref, ...), custom_call_target="tpu_custom_call" | custom-call | flops 2147483648 | bytes 4194304 | tf_op jit(solution)/shard_map/pallas_call | solution.py:398
  107.2 1.5 slice_add_fusion
  108.7 11.8 %shard_map.142 = (f32[1024,512]{1,0:T(8,128)}, bf16[1024,512]{1,0:T(8,128)(2,1)}) custom-call(bf16[1024,1792]{1,0:T(8,128)(2,1)} %get-tuple-element.27.p_ref, bf16[1024,1792]{1,0:T(8,128)(2,1)} %get-tuple-element.28.q_ref.q_hbm, bf16[1024,1792]{1,0:T(8,128)(2,1)} %bitcast.4.far_hbm.far_ref, bf16[3,1024,1024]{2,1,0:T(8,128)(2,1)} %get-tuple-element.33.e_ref, ...), custom_call_target="tpu_custom_call" | custom-call | flops 4294967296 | bytes 8388608 | tf_op jit(solution)/shard_map/pallas_call | solution.py:398
  120.5 19.5 %shard_map.143 = (f32[1024,1024]{1,0:T(8,128)}, bf16[1024,1024]{1,0:T(8,128)(2,1)}) custom-call(bf16[1024,1792]{1,0:T(8,128)(2,1)} %get-tuple-element.27.p_ref, bf16[1024,1792]{1,0:T(8,128)(2,1)} %get-tuple-element.28.q_ref.q_hbm, bf16[1024,1792]{1,0:T(8,128)(2,1)} %bitcast.4.far_hbm.far_ref, bf16[3,1024,1024]{2,1,0:T(8,128)(2,1)} %get-tuple-element.33.e_ref, ...), custom_call_target="tpu_custom_call" | custom-call | flops 8589934592 | bytes 16777216 | tf_op jit(solution)/shard_map/pallas_call | solution.py:398
  139.9 3.6 %all-to-all-done.2 = bf16[128,8,1792]{2,1,0:T(8,128)(2,1)} async-done(((bf16[128,8,1792]{2,1,0:T(8,128)(2,1)}), bf16[128,8,1792]{2,1,0:T(8,128)(2,1)}, u32[]{:S(2)}, u32[]{:S(2)}) %all-to-all-start.2) | async-done | bytes 3670048 | tf_op jit(solution)/shard_map/all_to_all | solution.py:32
  143.5 10.4 %shard_map.144 = (f32[1024,256]{1,0:T(8,128)}, f32[1024,512]{1,0:T(8,128)}, f32[1024,1024]{1,0:T(8,128)}) custom-call(s32[1,1024]{1,0:T(1,128)} %select_n.15.place_ref, bf16[1024,1792]{1,0:T(8,128)(2,1)} %bitcast.8.term_hbm, bf16[1024,256]{1,0:T(8,128)(2,1)} %get-tuple-element.41.part0, bf16[1024,512]{1,0:T(8,128)(2,1)} %get-tuple-element.42.part1, ...), custom_call_target="tpu_custom_call" | custom-call | flops 29360128 | bytes 22020096 | tf_op jit(solution)/shard_map/pallas_call | solution.py:429
Async XLA Ops:
  2.2 21.2 %all-to-all-start = ((s32[128,1,128]{2,1,0:T(1,128)}), s32[128,1,128]{2,1,0:T(1,128)S(1)}, u32[]{:S(2)}, u32[]{:S(2)}) async-start(s32[128,1,128]{2,1,0:T(1,128)} %bitcast.15), calls=%async_computation | async-start | bytes 131072 | tf_op jit(solution)/shard_map/all_to_all | solution.py:32
  23.4 0.6 copy-start
  28.1 5.6 %copy-start.2 = (s32[1024]{0:T(1024)S(1)}, s32[1024]{0:T(1024)}, u32[]{:S(2)}) copy-start(s32[1024]{0:T(1024)} %param.15) | copy-start | bytes 12292
  28.2 51.4 %all-to-all-start.1 = ((bf16[128,8,1792]{2,1,0:T(8,128)(2,1)}), bf16[128,8,1792]{2,1,0:T(8,128)(2,1)}, u32[]{:S(2)}, u32[]{:S(2)}) async-start(bf16[128,8,1792]{2,1,0:T(8,128)(2,1)} %bitcast.10), calls=%async_computation.1 | async-start | bytes 7340032 | tf_op jit(solution)/shard_map/all_to_all | solution.py:32
  92.0 5.6 %copy-start.1 = (s32[128,1,128]{2,1,0:T(1,128)S(1)}, s32[128,1,128]{2,1,0:T(1,128)}, u32[]{:S(2)}) copy-start(s32[128,1,128]{2,1,0:T(1,128)} %copy-done) | copy-start | bytes 196612
  92.0 51.5 %all-to-all-start.2 = ((bf16[128,8,1792]{2,1,0:T(8,128)(2,1)}), bf16[128,8,1792]{2,1,0:T(8,128)(2,1)}, u32[]{:S(2)}, u32[]{:S(2)}) async-start(bf16[128,8,1792]{2,1,0:T(8,128)(2,1)} %bitcast.11), calls=%async_computation.2 | async-start | bytes 7340032 | tf_op jit(solution)/shard_map/all_to_all | solution.py:32

commit v3 on v2

--- a/solution.py
+++ b/solution.py
@@ -131,10 +131,28 @@
         bias_ref[...] = bias
 
 
+def far_scratch(far, rows, wide):
+    return [
+        pltpu.VMEM((far, wide), BF16),
+        pltpu.VMEM((rows, wide), BF16),
+        pltpu.VMEM((far, LANES), F32),
+        pltpu.VMEM((8, rows), F32),
+        pltpu.VMEM((8, rows), F32),
+        pltpu.VMEM((8, rows), F32),
+        pltpu.VMEM((8, rows), F32),
+        pltpu.VMEM((far, rows), BF16),
+        pltpu.VMEM((far, rows), F32),
+        pltpu.VMEM((far, wide), BF16),
+        pltpu.SemaphoreType.DMA((4, 3)),
+        pltpu.SemaphoreType.DMA((4, 4)),
+    ]
+
+
 def far_kernel(
-    widths, starts, lists, far_hbm, q_hbm, bias_ref, tot_ref, spos_ref,
-    term_hbm, scale_ref, loss_ref,
-    far_ref, q_ref, g_ref, e_v, term_v, in_sems, out_sems,
+    widths, starts, lists, far_hbm, q_hbm, bias_hbm, tot_hbm, spos_hbm,
+    term_hbm, scale_hbm, loss_hbm,
+    far_ref, q_ref, bias_ref, tot_ref, spos_ref, scale_ref, loss_ref,
+    g_ref, e_v, term_v, in_sems, out_sems,
 ):
     far, rows = g_ref.shape
     cols = rows // lists
@@ -143,14 +161,21 @@
     loads = {}
     for k in order:
         span = pl.ds(starts[k], widths[k])
-        loads[k] = (
+        loads[k] = [
             pltpu.make_async_copy(far_hbm.at[:, span], far_ref.at[:, span], in_sems.at[k, 0]),
             pltpu.make_async_copy(q_hbm.at[:, span], q_ref.at[:, span], in_sems.at[k, 1]),
-        )
+        ]
+        if k == order[0]:
+            loads[k] += [
+                pltpu.make_async_copy(bias_hbm, bias_ref, in_sems.at[3, 0]),
+                pltpu.make_async_copy(tot_hbm, tot_ref, in_sems.at[3, 1]),
+                pltpu.make_async_copy(spos_hbm, spos_ref, in_sems.at[3, 2]),
+            ]
         for load in loads[k]:
             load.start()
+    scale_ref[3:8, :] = jnp.zeros((5, rows), F32)
+    loss_ref[3:8, :] = jnp.zeros((5, rows), F32)
     stores = []
-    step = 256
     for k in order:
         span = slice(starts[k], starts[k] + widths[k])
         for load in loads[k]:
@@ -170,14 +195,19 @@
             loss_ref[k : k + 1, at_q] = jnp.log(tot) - spos_ref[k : k + 1, at_q]
             for at in range(0, far, chunk):
                 g_ref[at : at + chunk, at_q] = (e_v[at : at + chunk, at_q] * scale).astype(BF16)
-        for at in range(starts[k], starts[k] + widths[k], step):
-            here = slice(at, at + step)
-            for row in range(0, far, chunk):
-                part = jnp.dot(g_ref[row : row + chunk, :], q_ref[:, here], preferred_element_type=F32)
-                term_v[row : row + chunk, here] = part.astype(BF16)
-            here = pl.ds(at, step)
+        if k == order[-1]:
+            for index, (ref, hbm) in enumerate(((scale_ref, scale_hbm), (loss_ref, loss_hbm))):
+                stores.append(pltpu.make_async_copy(ref, hbm, out_sems.at[3, index]))
+                stores[-1].start()
+        for row in range(0, far, chunk):
+            here = slice(row, row + chunk)
+            part = jnp.dot(g_ref[here, :], q_ref[:, span], preferred_element_type=F32)
+            unit = far_ref[here, span].astype(F32)
+            part = part - unit * jnp.sum(unit * part, axis=1, keepdims=True)
+            term_v[here, span] = part.astype(BF16)
+            place = (pl.ds(row, chunk), pl.ds(starts[k], widths[k]))
             store = pltpu.make_async_copy(
-                term_v.at[:, here], term_hbm.at[:, here], out_sems.at[at // step]
+                term_v.at[place], term_hbm.at[place], out_sems.at[k, row // chunk]
             )
             store.start()
             stores.append(store)
@@ -238,27 +268,48 @@
             part_ref[here, :] = part.astype(BF16)
 
 
+def passage_scratch(widths, far, rows, wide):
+    return (
+        [
+            pltpu.VMEM((far, wide), BF16),
+            pltpu.VMEM((rows, far), BF16),
+            pltpu.VMEM((rows, LANES), F32),
+            pltpu.VMEM((8, far), jnp.int32),
+        ]
+        + [pltpu.VMEM((rows, width), BF16) for width in widths]
+        + [pltpu.VMEM((rows, width), F32) for width in widths]
+        + [pltpu.SemaphoreType.DMA((4, 3)), pltpu.SemaphoreType.DMA((3, 4))]
+    )
+
+
 def passage_kernel(
-    widths, starts, place_ref, term_hbm, part0, part1, part2, raw0, raw1, raw2, inv_ref,
+    widths, starts, place_hbm, term_hbm, part0, part1, part2, inv_hbm,
     out0, out1, out2,
-    term_v, pick_v, dv0, dv1, dv2, rv0, rv1, rv2, ov0, ov1, ov2, in_sems, out_sems,
+    term_v, pick_v, inv_ref, place_ref, pv0, pv1, pv2, ov0, ov1, ov2, in_sems, out_sems,
 ):
-    parts, raws, outs = (part0, part1, part2), (raw0, raw1, raw2), (out0, out1, out2)
-    part_vs, raw_vs, out_vs = (dv0, dv1, dv2), (rv0, rv1, rv2), (ov0, ov1, ov2)
+    parts, outs = (part0, part1, part2), (out0, out1, out2)
+    part_vs, out_vs = (pv0, pv1, pv2), (ov0, ov1, ov2)
     rows = ov0.shape[0]
     far = term_v.shape[0]
     order = (0, 1, 2)
     chunk = min(256, rows)
+    small = (
+        pltpu.make_async_copy(place_hbm, place_ref, in_sems.at[3, 0]),
+        pltpu.make_async_copy(inv_hbm, inv_ref, in_sems.at[3, 1]),
+    )
+    for load in small:
+        load.start()
     loads = {}
     for k in order:
         span = pl.ds(starts[k], widths[k])
         loads[k] = (
             pltpu.make_async_copy(term_hbm.at[:, span], term_v.at[:, span], in_sems.at[k, 0]),
             pltpu.make_async_copy(parts[k], part_vs[k], in_sems.at[k, 1]),
-            pltpu.make_async_copy(raws[k], raw_vs[k], in_sems.at[k, 2]),
         )
         for load in loads[k]:
             load.start()
+    for load in small:
+        load.wait()
     place = place_ref[0:1, :]
     for at in range(0, rows, chunk):
         row = lax.broadcasted_iota(jnp.int32, (chunk, far), 0) + at
@@ -272,7 +323,7 @@
             here = slice(at, at + chunk)
             inverse = inv_ref[here, k : k + 1]
             added = jnp.dot(pick_v[here, :], terms, preferred_element_type=F32)
-            added = raw_gradient(raw_vs[k][here, :], inverse, added)
+            added = added * inverse
             out_vs[k][here, :] = part_vs[k][here, :].astype(F32) + added
             part = pl.ds(at, chunk)
             store = pltpu.make_async_copy(
@@ -373,17 +424,9 @@
     terms, scales, loss_rows = pl.pallas_call(
         functools.partial(far_kernel, widths, starts, lists),
         out_shape=(shape((far, wide), BF16), shape((8, rows), F32), shape((8, rows), F32)),
-        in_specs=[HBM, HBM, VMEM, VMEM, VMEM],
-        out_specs=(HBM, VMEM, VMEM),
-        scratch_shapes=[
-            pltpu.VMEM((far, wide), BF16),
-            pltpu.VMEM((rows, wide), BF16),
-            pltpu.VMEM((far, rows), BF16),
-            pltpu.VMEM((far, rows), F32),
-            pltpu.VMEM((far, wide), BF16),
-            pltpu.SemaphoreType.DMA((3, 2)),
-            pltpu.SemaphoreType.DMA((wide // 256,)),
-        ],
+        in_specs=[HBM] * 5,
+        out_specs=(HBM,) * 3,
+        scratch_shapes=far_scratch(far, rows, wide),
         compiler_params=params,
         cost_estimate=cost(4 * far * rows * wide, 6 * far * wide),
     )(fetched, q_all, bias, totals, positive_scores)
@@ -426,19 +469,16 @@
     offsets = jnp.arange(PROWS, dtype=jnp.int32)
     asked_ids = asked[:, :1]
     place = jnp.where(asked_ids >= 0, asked_ids * PROWS + offsets[None, :], -1).reshape(1, far)
+    place = jnp.broadcast_to(place, (8, far))
     p_grads = pl.pallas_call(
         functools.partial(passage_kernel, widths, starts),
         out_shape=tuple(shape((rows, width), F32) for width in widths),
-        in_specs=[VMEM] + [HBM] * 7 + [VMEM],
-        out_specs=(HBM, HBM, HBM),
-        scratch_shapes=[pltpu.VMEM((far, wide), BF16), pltpu.VMEM((rows, far), BF16)]
-        + [pltpu.VMEM((rows, width), BF16) for width in widths]
-        + [pltpu.VMEM((rows, width), BF16) for width in widths]
-        + [pltpu.VMEM((rows, width), F32) for width in widths]
-        + [pltpu.SemaphoreType.DMA((3, 3)), pltpu.SemaphoreType.DMA((3, 4))],
+        in_specs=[HBM] * 6,
+        out_specs=(HBM,) * 3,
+        scratch_shapes=passage_scratch(widths, far, rows, wide),
         compiler_params=params,
         cost_estimate=cost(16 * rows * wide, 12 * rows * wide),
-    )(place, returned, *p_parts, *passages, p_inverses)
+    )(place, returned, *p_parts, p_inverses)
     return (losses, *q_grads, *p_grads)
 
 

time: 155 us -> 152 us (0.981)
  Pallas kernels: 88.8 us -> 84.8 us
    pallas_call x1, Pallas kernels: 10.4 us -> 7.38 us  [local(): pl.pallas_call(functools.partial(passage_kernel, widths, starts), out_sha...]
  transfers between devices with their start and end apart: 3 -> 3, of which waited for: 3 -> 3; matrix products, arithmetic and copies ran while one was open for 2% -> 2% of each run, Pallas kernels for 39% -> 40%
where the time goes in v3:
time: 152 us; the launch traced here: 151 us
  Pallas kernels  84.8 us (56%)
  waiting for transfers between devices  38.6 us (25%)
  starting transfers between devices  22.7 us (15%)
  other arithmetic  2.39 us (2%)
    pallas_call x3, Pallas kernels, local(): pl.pallas_call(functools.partial(near_kernel, k, lists), grid=(lists,), o...  39.9 us
    all_to_all x3, waiting for transfers between devices, exchange(): return lax.all_to_all(values, AXES, split_axis=0, concat_axis=0, tiled=True)  38.6 us
    all_to_all x3, starting transfers between devices, exchange(): return lax.all_to_all(values, AXES, split_axis=0, concat_axis=0, tiled=True)  22.7 us
    pallas_call x1, Pallas kernels, local(): pl.pallas_call(functools.partial(far_kernel, widths, starts, lists), out_...  11.5 us
    pallas_call x1, Pallas kernels, local(): pl.pallas_call(functools.partial(local_kernel, widths, starts, block_coun...  10.3 us
    pallas_call x2, Pallas kernels, heads(): pl.pallas_call(functools.partial(heads_kernel, widths, starts), grid=(4,)...  10.2 us
    pallas_call x1, Pallas kernels, local(): pl.pallas_call(functools.partial(passage_kernel, widths, starts), out_sha...  7.38 us
    pallas_call x1, Pallas kernels, local(): pl.pallas_call(gather_kernel, out_shape=shape((far, wide), BF16), in_spec...  4.06 us
  transfers between devices with their start and end apart: 3, of which 3 were waited for; matrix products, arithmetic and copies ran while one was open for 2% of the time, Pallas kernels for 40%

profile of v3, /device:TPU:1, one launch (start us, length us, event | category | flops | bytes accessed | tf_op | source)
XLA Modules:
  0.0 150.7 jit_solution(6190751145843163505)
XLA Ops:
  0.6 1.6 %shard_map.135.after_ref = s32[128,128]{1,0:T(8,128)} custom-call(s32[4,127]{1,0:T(4,128)} %neg_ref.3), custom_call_target="tpu_custom_call" | custom-call | tf_op jit(solution)/shard_map/pallas_call | solution.py:358
  2.2 11.5 %all-to-all-start = ((s32[128,1,128]{2,1,0:T(1,128)}), s32[128,1,128]{2,1,0:T(1,128)S(1)}, u32[]{:S(2)}, u32[]{:S(2)}) async-start(s32[128,1,128]{2,1,0:T(1,128)} %bitcast.15), calls=%async_computation | async-start | bytes 131072 | tf_op jit(solution)/shard_map/all_to_all | solution.py:32
  13.7 5.1 %shard_map.136 = (bf16[1024,1792]{1,0:T(8,128)(2,1)}, f32[1024,128]{1,0:T(8,128)}) custom-call(bf16[1024,256]{1,0:T(8,128)(2,1)} %p_raw_ref.3, bf16[1024,512]{1,0:T(8,128)(2,1)} %p_raw_ref.4, bf16[1024,1024]{1,0:T(8,128)(2,1)} %p_raw_ref.5, s32[128,128]{1,0:T(8,128)} %shard_map.135.after_ref), custom_call_target="tpu_custom_call" | custom-call | flops 7340032 | bytes 7340032 | tf_op jit(solution)/shard_map/pallas_call | solution.py:371
  18.8 4.6 %all-to-all-done = s32[128,1,128]{2,1,0:T(1,128)S(1)} async-done(((s32[128,1,128]{2,1,0:T(1,128)}), s32[128,1,128]{2,1,0:T(1,128)S(1)}, u32[]{:S(2)}, u32[]{:S(2)}) %all-to-all-start) | async-done | bytes 65568 | tf_op jit(solution)/shard_map/all_to_all | solution.py:32
  23.4 0.0 copy-start
  23.4 0.6 copy-done
  24.1 4.1 %shard_map.137.after_ref = bf16[1024,1792]{1,0:T(8,128)(2,1)} custom-call(s32[128,128]{1,0:T(8,128)} %bitcast.12, bf16[1024,1792]{1,0:T(8,128)(2,1)} %get-tuple-element.27.p_ref), custom_call_target="tpu_custom_call" | custom-call | flops 1835008 | bytes 7340032 | tf_op jit(solution)/shard_map/pallas_call | solution.py:383
  28.1 0.0 copy-start.2
  28.2 5.6 %all-to-all-start.1 = ((bf16[128,8,1792]{2,1,0:T(8,128)(2,1)}), bf16[128,8,1792]{2,1,0:T(8,128)(2,1)}, u32[]{:S(2)}, u32[]{:S(2)}) async-start(bf16[128,8,1792]{2,1,0:T(8,128)(2,1)} %bitcast.10), calls=%async_computation.1 | async-start | bytes 7340032 | tf_op jit(solution)/shard_map/all_to_all | solution.py:32
  33.7 0.0 copy-done.2
  33.8 0.6 broadcast_subtract_fusion
  34.3 5.1 %shard_map.138 = (bf16[1024,1792]{1,0:T(8,128)(2,1)}, f32[1024,128]{1,0:T(8,128)}) custom-call(bf16[1024,256]{1,0:T(8,128)(2,1)} %raw_ref.3, bf16[1024,512]{1,0:T(8,128)(2,1)} %raw_ref.4, bf16[1024,1024]{1,0:T(8,128)(2,1)} %raw_ref.5, bf16[1024,1792]{1,0:T(8,128)(2,1)} %shard_map.137.after_ref), custom_call_target="tpu_custom_call" | custom-call | flops 7340032 | bytes 7340032 | tf_op jit(solution)/shard_map/pallas_call | solution.py:371
  39.4 10.3 %shard_map.139 = (f32[8,1024]{1,0:T(8,128)}, f32[8,1024]{1,0:T(8,128)}, f32[1024,128]{1,0:T(8,128)}, bf16[3,1024,1024]{2,1,0:T(8,128)(2,1)}) custom-call(bf16[1024,1792]{1,0:T(8,128)(2,1)} %get-tuple-element.27.p_ref, bf16[1024,1792]{1,0:T(8,128)(2,1)} %get-tuple-element.28.q_ref.q_hbm, s32[1,1024]{1,0:T(1,128)} %bitcast.16, s32[4,127]{1,0:T(4,128)} %neg_ref.3), custom_call_target="tpu_custom_call" | custom-call | flops 3758096384 | bytes 7340032 | tf_op jit(solution)/shard_map/pallas_call | solution.py:399
  49.7 29.8 %all-to-all-done.1 = bf16[128,8,1792]{2,1,0:T(8,128)(2,1)} async-done(((bf16[128,8,1792]{2,1,0:T(8,128)(2,1)}), bf16[128,8,1792]{2,1,0:T(8,128)(2,1)}, u32[]{:S(2)}, u32[]{:S(2)}) %all-to-all-start.1) | async-done | bytes 3670048 | tf_op jit(solution)/shard_map/all_to_all | solution.py:32
  79.5 11.5 %shard_map.140 = (bf16[1024,1792]{1,0:T(8,128)(2,1)}, f32[8,1024]{1,0:T(8,128)}, f32[8,1024]{1,0:T(8,128)}) custom-call(bf16[1024,1792]{1,0:T(8,128)(2,1)} %bitcast.4.far_hbm.far_ref, bf16[1024,1792]{1,0:T(8,128)(2,1)} %get-tuple-element.28.q_ref.q_hbm, f32[1024,128]{1,0:T(8,128)} %get-tuple-element.29.bias_hbm.bias_ref, ...), custom_call_target="tpu_custom_call" | custom-call | flops 7516192768 | bytes 11010048 | tf_op jit(solution)/shard_map/pallas_call | solution.py:424
  91.0 0.0 copy-start.1
  91.0 5.6 %all-to-all-start.2 = ((bf16[128,8,1792]{2,1,0:T(8,128)(2,1)}), bf16[128,8,1792]{2,1,0:T(8,128)(2,1)}, u32[]{:S(2)}, u32[]{:S(2)}) async-start(bf16[128,8,1792]{2,1,0:T(8,128)(2,1)} %bitcast.11), calls=%async_computation.2 | async-start | bytes 7340032 | tf_op jit(solution)/shard_map/all_to_all | solution.py:32
  96.6 0.0 copy-done.1
  96.6 0.1 multiply_reduce_fusion
  96.7 0.1 compare_reduce_fusion
  96.9 0.1 add_select_fusion
  97.0 0.1 select_n.12
  97.1 8.6 %shard_map.141 = (f32[1024,256]{1,0:T(8,128)}, bf16[1024,256]{1,0:T(8,128)(2,1)}) custom-call(bf16[1024,1792]{1,0:T(8,128)(2,1)} %get-tuple-element.27.p_ref, bf16[1024,1792]{1,0:T(8,128)(2,1)} %get-tuple-element.28.q_ref.q_hbm, bf16[1024,1792]{1,0:T(8,128)(2,1)} %bitcast.4.far_hbm.far_ref, bf16[3,1024,1024]{2,1,0:T(8,128)(2,1)} %get-tuple-element.33.e_ref, ...), custom_call_target="tpu_custom_call" | custom-call | flops 2147483648 | bytes 4194304 | tf_op jit(solution)/shard_map/pallas_call | solution.py:441
  105.7 1.5 slice_add_fusion
  107.2 11.8 %shard_map.142 = (f32[1024,512]{1,0:T(8,128)}, bf16[1024,512]{1,0:T(8,128)(2,1)}) custom-call(bf16[1024,1792]{1,0:T(8,128)(2,1)} %get-tuple-element.27.p_ref, bf16[1024,1792]{1,0:T(8,128)(2,1)} %get-tuple-element.28.q_ref.q_hbm, bf16[1024,1792]{1,0:T(8,128)(2,1)} %bitcast.4.far_hbm.far_ref, bf16[3,1024,1024]{2,1,0:T(8,128)(2,1)} %get-tuple-element.33.e_ref, ...), custom_call_target="tpu_custom_call" | custom-call | flops 4294967296 | bytes 8388608 | tf_op jit(solution)/shard_map/pallas_call | solution.py:441
  119.0 19.5 %shard_map.143 = (f32[1024,1024]{1,0:T(8,128)}, bf16[1024,1024]{1,0:T(8,128)(2,1)}) custom-call(bf16[1024,1792]{1,0:T(8,128)(2,1)} %get-tuple-element.27.p_ref, bf16[1024,1792]{1,0:T(8,128)(2,1)} %get-tuple-element.28.q_ref.q_hbm, bf16[1024,1792]{1,0:T(8,128)(2,1)} %bitcast.4.far_hbm.far_ref, bf16[3,1024,1024]{2,1,0:T(8,128)(2,1)} %get-tuple-element.33.e_ref, ...), custom_call_target="tpu_custom_call" | custom-call | flops 8589934592 | bytes 16777216 | tf_op jit(solution)/shard_map/pallas_call | solution.py:441
  138.4 4.1 %all-to-all-done.2 = bf16[128,8,1792]{2,1,0:T(8,128)(2,1)} async-done(((bf16[128,8,1792]{2,1,0:T(8,128)(2,1)}), bf16[128,8,1792]{2,1,0:T(8,128)(2,1)}, u32[]{:S(2)}, u32[]{:S(2)}) %all-to-all-start.2) | async-done | bytes 3670048 | tf_op jit(solution)/shard_map/all_to_all | solution.py:32
  142.5 0.6 broadcast_in_dim.27.place_hbm
  143.1 7.4 %shard_map.144 = (f32[1024,256]{1,0:T(8,128)}, f32[1024,512]{1,0:T(8,128)}, f32[1024,1024]{1,0:T(8,128)}) custom-call(s32[8,1024]{1,0:T(8,128)} %broadcast_in_dim.27.place_hbm, bf16[1024,1792]{1,0:T(8,128)(2,1)} %bitcast.8.term_hbm, bf16[1024,256]{1,0:T(8,128)(2,1)} %get-tuple-element.41.part0, bf16[1024,512]{1,0:T(8,128)(2,1)} %get-tuple-element.42.part1, ...), custom_call_target="tpu_custom_call" | custom-call | flops 29360128 | bytes 22020096 | tf_op jit(solution)/shard_map/pallas_call | solution.py:473
Async XLA Ops:
  2.2 21.2 %all-to-all-start = ((s32[128,1,128]{2,1,0:T(1,128)}), s32[128,1,128]{2,1,0:T(1,128)S(1)}, u32[]{:S(2)}, u32[]{:S(2)}) async-start(s32[128,1,128]{2,1,0:T(1,128)} %bitcast.15), calls=%async_computation | async-start | bytes 131072 | tf_op jit(solution)/shard_map/all_to_all | solution.py:32
  23.4 0.6 copy-start
  28.1 5.6 %copy-start.2 = (s32[1024]{0:T(1024)S(1)}, s32[1024]{0:T(1024)}, u32[]{:S(2)}) copy-start(s32[1024]{0:T(1024)} %param.15) | copy-start | bytes 12292
  28.2 51.4 %all-to-all-start.1 = ((bf16[128,8,1792]{2,1,0:T(8,128)(2,1)}), bf16[128,8,1792]{2,1,0:T(8,128)(2,1)}, u32[]{:S(2)}, u32[]{:S(2)}) async-start(bf16[128,8,1792]{2,1,0:T(8,128)(2,1)} %bitcast.10), calls=%async_computation.1 | async-start | bytes 7340032 | tf_op jit(solution)/shard_map/all_to_all | solution.py:32
  91.0 5.6 %copy-start.1 = (s32[128,1,128]{2,1,0:T(1,128)S(1)}, s32[128,1,128]{2,1,0:T(1,128)}, u32[]{:S(2)}) copy-start(s32[128,1,128]{2,1,0:T(1,128)} %copy-done) | copy-start | bytes 196612
  91.0 51.5 %all-to-all-start.2 = ((bf16[128,8,1792]{2,1,0:T(8,128)(2,1)}), bf16[128,8,1792]{2,1,0:T(8,128)(2,1)}, u32[]{:S(2)}, u32[]{:S(2)}) async-start(bf16[128,8,1792]{2,1,0:T(8,128)(2,1)} %bitcast.11), calls=%async_computation.2 | async-start | bytes 7340032 | tf_op jit(solution)/shard_map/all_to_all | solution.py:32

commit v4 on v3

--- a/solution.py
+++ b/solution.py
@@ -70,22 +70,26 @@
     inv_ref[...] = packed
 
 
-def gather_kernel(asked_ref, p_ref, out_hbm, out_v, sems):
+def gather_kernel(widths, starts, asked_ref, raw0, raw1, raw2, out_hbm, out_v, sems):
+    raws = (raw0, raw1, raw2)
     pairs = out_v.shape[0] // 16
     parts = min(8, pairs)
     each = pairs // parts
 
-    def block(peer):
+    def block(raw, peer):
         ident = jnp.maximum(asked_ref[peer, 0], 0)
         start = pl.multiple_of((ident // 2) * 16, 16)
-        both = p_ref[pl.ds(start, 16), :].astype(F32)
+        both = raw[pl.ds(start, 16), :].astype(F32)
         return jnp.where(ident % 2 == 0, both[:8], both[8:])
 
     stores = []
     for part in range(parts):
         for pair in range(part * each, (part + 1) * each):
-            rows = jnp.concatenate([block(pair * 2), block(pair * 2 + 1)], axis=0)
-            out_v[pair * 16 : pair * 16 + 16, :] = rows.astype(BF16)
+            for k in range(3):
+                values = jnp.concatenate([block(raws[k], pair * 2), block(raws[k], pair * 2 + 1)], axis=0)
+                inverse = lax.rsqrt(jnp.sum(values * values, axis=1, keepdims=True) + EPSILON)
+                place = slice(starts[k], starts[k] + widths[k])
+                out_v[pair * 16 : pair * 16 + 16, place] = (values * inverse).astype(BF16)
         here = pl.ds(part * each * 16, each * 16)
         store = pltpu.make_async_copy(out_v.at[here, :], out_hbm.at[here, :], sems.at[part])
         store.start()
@@ -274,7 +278,7 @@
             pltpu.VMEM((far, wide), BF16),
             pltpu.VMEM((rows, far), BF16),
             pltpu.VMEM((rows, LANES), F32),
-            pltpu.VMEM((8, far), jnp.int32),
+            pltpu.VMEM((1, far), jnp.int32),
         ]
         + [pltpu.VMEM((rows, width), BF16) for width in widths]
         + [pltpu.VMEM((rows, width), F32) for width in widths]
@@ -310,7 +314,7 @@
             load.start()
     for load in small:
         load.wait()
-    place = place_ref[0:1, :]
+    place = place_ref[...]
     for at in range(0, rows, chunk):
         row = lax.broadcasted_iota(jnp.int32, (chunk, far), 0) + at
         pick_v[at : at + chunk, :] = jnp.where(row == place, 1.0, 0.0).astype(BF16)
@@ -378,19 +382,18 @@
             cost_estimate=cost(rows * wide * 4, rows * wide * 4),
         )(*values, after)
 
-    p_all, p_inverses = heads(passages, wanted)
-
     send = pl.pallas_call(
-        gather_kernel,
+        functools.partial(gather_kernel, widths, starts),
         out_shape=shape((far, wide), BF16),
-        in_specs=[SMEM, VMEM],
+        in_specs=[SMEM, VMEM, VMEM, VMEM],
         out_specs=HBM,
         scratch_shapes=[pltpu.VMEM((far, wide), BF16), pltpu.SemaphoreType.DMA((8,))],
-        compiler_params=params,
-        cost_estimate=cost(far * wide, far * wide * 4),
-    )(asked, p_all)
+        compiler_params=pltpu.CompilerParams(vmem_limit_bytes=62 * MIB),
+        cost_estimate=cost(far * wide * 4, far * wide * 4),
+    )(asked, *passages)
     fetched = exchange(send.reshape(devices, PROWS, wide)).reshape(far, wide)
 
+    p_all, p_inverses = heads(passages, send)
     q_all, q_inverses = heads(queries, send)
     local_pos = (positives - own * rows).reshape(1, rows)
     whole = lambda dims: pl.BlockSpec(dims, lambda i: (0,) * len(dims))
@@ -469,7 +472,6 @@
     offsets = jnp.arange(PROWS, dtype=jnp.int32)
     asked_ids = asked[:, :1]
     place = jnp.where(asked_ids >= 0, asked_ids * PROWS + offsets[None, :], -1).reshape(1, far)
-    place = jnp.broadcast_to(place, (8, far))
     p_grads = pl.pallas_call(
         functools.partial(passage_kernel, widths, starts),
         out_shape=tuple(shape((rows, width), F32) for width in widths),

time: 152 us -> 151 us (level)
  blocking collectives: 0 us -> 21.6 us
  starting transfers between devices: 22.7 us -> 11 us
  waiting for transfers between devices: 38.6 us -> 28.5 us
    all_to_all x0 -> x1, blocking collectives: none -> 21.6 us  [exchange(): return lax.all_to_all(values, AXES, split_axis=0, concat_axis=0, tiled=True)]
    all_to_all x3 -> x2, starting transfers between devices: 22.7 us -> 11 us  [exchange(): return lax.all_to_all(values, AXES, split_axis=0, concat_axis=0, tiled=True)]
    all_to_all x3 -> x2, waiting for transfers between devices: 38.6 us -> 28.5 us  [exchange(): return lax.all_to_all(values, AXES, split_axis=0, concat_axis=0, tiled=True)]
  transfers between devices with their start and end apart: 3 -> 2, of which waited for: 3 -> 2; matrix products, arithmetic and copies ran while one was open for 2% -> 2% of each run, Pallas kernels for 40% -> 40%
where the time goes in v4:
time: 151 us; the launch traced here: 150 us
  Pallas kernels  85.3 us (56%)
  waiting for transfers between devices  28.5 us (19%)
  blocking collectives  21.6 us (14%)
  starting transfers between devices  11 us (7%)
  other arithmetic  2.39 us (2%)
    pallas_call x3, Pallas kernels, local(): pl.pallas_call(functools.partial(near_kernel, k, lists), grid=(lists,), o...  39.8 us
    all_to_all x2, waiting for transfers between devices, exchange(): return lax.all_to_all(values, AXES, split_axis=0, concat_axis=0, tiled=True)  28.5 us
    all_to_all x1, blocking collectives, exchange(): return lax.all_to_all(values, AXES, split_axis=0, concat_axis=0, tiled=True)  21.6 us
    pallas_call x1, Pallas kernels, local(): pl.pallas_call(functools.partial(far_kernel, widths, starts, lists), out_...  11.4 us
    all_to_all x2, starting transfers between devices, exchange(): return lax.all_to_all(values, AXES, split_axis=0, concat_axis=0, tiled=True)  11 us
    pallas_call x1, Pallas kernels, local(): pl.pallas_call(functools.partial(local_kernel, widths, starts, block_coun...  10.3 us
    pallas_call x2, Pallas kernels, heads(): pl.pallas_call(functools.partial(heads_kernel, widths, starts), grid=(4,)...  10.2 us
    pallas_call x1, Pallas kernels, local(): pl.pallas_call(functools.partial(passage_kernel, widths, starts), out_sha...  7.25 us
  transfers between devices with their start and end apart: 2, of which 2 were waited for; matrix products, arithmetic and copies ran while one was open for 2% of the time, Pallas kernels for 40%

profile of v4, /device:TPU:1, one launch (start us, length us, event | category | flops | bytes accessed | tf_op | source)
XLA Modules:
  0.0 150.4 jit_solution(3635163043304992011)
XLA Ops:
  0.6 1.6 %shard_map.135 = s32[128,128]{1,0:T(8,128)} custom-call(s32[4,127]{1,0:T(4,128)} %neg_ref.3), custom_call_target="tpu_custom_call" | custom-call | tf_op jit(solution)/shard_map/pallas_call | solution.py:362
  2.2 21.6 %all_to_all.15 = s32[128,1,128]{2,1,0:T(1,128)} all-to-all(s32[128,1,128]{2,1,0:T(1,128)} %bitcast.15), channel_id=1, replica_groups=mesh['dp'=8,'group'=16] {'dp','group'}, dimensions={0} | all-to-all | bytes 131072 | tf_op jit(solution)/shard_map/all_to_all | solution.py:32
  23.8 4.7 %shard_map.136.after_ref = bf16[1024,1792]{1,0:T(8,128)(2,1)} custom-call(s32[128,128]{1,0:T(8,128)} %bitcast.12, bf16[1024,256]{1,0:T(8,128)(2,1)} %p_raw_ref.3, bf16[1024,512]{1,0:T(8,128)(2,1)} %p_raw_ref.4, bf16[1024,1024]{1,0:T(8,128)(2,1)} %p_raw_ref.5), custom_call_target="tpu_custom_call" | custom-call | flops 7340032 | bytes 7340032 | tf_op jit(solution)/shard_map/pallas_call | solution.py:385
  28.5 0.0 copy-start.1
  28.5 5.5 %all-to-all-start.1 = ((bf16[128,8,1792]{2,1,0:T(8,128)(2,1)}), bf16[128,8,1792]{2,1,0:T(8,128)(2,1)}, u32[]{:S(2)}, u32[]{:S(2)}) async-start(bf16[128,8,1792]{2,1,0:T(8,128)(2,1)} %bitcast.10), calls=%async_computation.1 | async-start | bytes 7340032 | tf_op jit(solution)/shard_map/all_to_all | solution.py:32
  34.0 0.0 copy-done.1
  34.0 0.6 broadcast_subtract_fusion
  34.6 5.1 %shard_map.138 = (bf16[1024,1792]{1,0:T(8,128)(2,1)}, f32[1024,128]{1,0:T(8,128)}) custom-call(bf16[1024,256]{1,0:T(8,128)(2,1)} %p_raw_ref.3, bf16[1024,512]{1,0:T(8,128)(2,1)} %p_raw_ref.4, bf16[1024,1024]{1,0:T(8,128)(2,1)} %p_raw_ref.5, bf16[1024,1792]{1,0:T(8,128)(2,1)} %shard_map.136.after_ref), custom_call_target="tpu_custom_call" | custom-call | flops 7340032 | bytes 7340032 | tf_op jit(solution)/shard_map/pallas_call | solution.py:375
  39.7 5.1 %shard_map.137 = (bf16[1024,1792]{1,0:T(8,128)(2,1)}, f32[1024,128]{1,0:T(8,128)}) custom-call(bf16[1024,256]{1,0:T(8,128)(2,1)} %raw_ref.3, bf16[1024,512]{1,0:T(8,128)(2,1)} %raw_ref.4, bf16[1024,1024]{1,0:T(8,128)(2,1)} %raw_ref.5, bf16[1024,1792]{1,0:T(8,128)(2,1)} %shard_map.136.after_ref), custom_call_target="tpu_custom_call" | custom-call | flops 7340032 | bytes 7340032 | tf_op jit(solution)/shard_map/pallas_call | solution.py:375
  44.8 10.3 %shard_map.139 = (f32[8,1024]{1,0:T(8,128)}, f32[8,1024]{1,0:T(8,128)}, f32[1024,128]{1,0:T(8,128)}, bf16[3,1024,1024]{2,1,0:T(8,128)(2,1)}) custom-call(bf16[1024,1792]{1,0:T(8,128)(2,1)} %get-tuple-element.28.p_ref, bf16[1024,1792]{1,0:T(8,128)(2,1)} %get-tuple-element.27.q_ref.q_hbm, s32[1,1024]{1,0:T(1,128)} %bitcast.16, s32[4,127]{1,0:T(4,128)} %neg_ref.3), custom_call_target="tpu_custom_call" | custom-call | flops 3758096384 | bytes 7340032 | tf_op jit(solution)/shard_map/pallas_call | solution.py:402
  55.1 24.9 %all-to-all-done.1 = bf16[128,8,1792]{2,1,0:T(8,128)(2,1)} async-done(((bf16[128,8,1792]{2,1,0:T(8,128)(2,1)}), bf16[128,8,1792]{2,1,0:T(8,128)(2,1)}, u32[]{:S(2)}, u32[]{:S(2)}) %all-to-all-start.1) | async-done | bytes 3670048 | tf_op jit(solution)/shard_map/all_to_all | solution.py:32
  80.0 11.4 %shard_map.140 = (bf16[1024,1792]{1,0:T(8,128)(2,1)}, f32[8,1024]{1,0:T(8,128)}, f32[8,1024]{1,0:T(8,128)}) custom-call(bf16[1024,1792]{1,0:T(8,128)(2,1)} %bitcast.4.far_hbm.far_ref, bf16[1024,1792]{1,0:T(8,128)(2,1)} %get-tuple-element.27.q_ref.q_hbm, f32[1024,128]{1,0:T(8,128)} %get-tuple-element.29.bias_hbm.bias_ref, ...), custom_call_target="tpu_custom_call" | custom-call | flops 7516192768 | bytes 11010048 | tf_op jit(solution)/shard_map/pallas_call | solution.py:427
  91.4 0.0 copy-start
  91.4 5.6 %all-to-all-start.2 = ((bf16[128,8,1792]{2,1,0:T(8,128)(2,1)}), bf16[128,8,1792]{2,1,0:T(8,128)(2,1)}, u32[]{:S(2)}, u32[]{:S(2)}) async-start(bf16[128,8,1792]{2,1,0:T(8,128)(2,1)} %bitcast.11), calls=%async_computation.2 | async-start | bytes 7340032 | tf_op jit(solution)/shard_map/all_to_all | solution.py:32
  97.0 0.0 copy-done
  97.0 0.1 multiply_reduce_fusion
  97.1 0.1 compare_reduce_fusion
  97.2 0.1 add_select_fusion
  97.4 0.7 select_n.15.place_hbm
  98.0 8.6 %shard_map.141 = (f32[1024,256]{1,0:T(8,128)}, bf16[1024,256]{1,0:T(8,128)(2,1)}) custom-call(bf16[1024,1792]{1,0:T(8,128)(2,1)} %get-tuple-element.28.p_ref, bf16[1024,1792]{1,0:T(8,128)(2,1)} %get-tuple-element.27.q_ref.q_hbm, bf16[1024,1792]{1,0:T(8,128)(2,1)} %bitcast.4.far_hbm.far_ref, bf16[3,1024,1024]{2,1,0:T(8,128)(2,1)} %get-tuple-element.33.e_ref, ...), custom_call_target="tpu_custom_call" | custom-call | flops 2147483648 | bytes 4194304 | tf_op jit(solution)/shard_map/pallas_call | solution.py:444
  106.7 1.5 slice_add_fusion
  108.1 11.8 %shard_map.142 = (f32[1024,512]{1,0:T(8,128)}, bf16[1024,512]{1,0:T(8,128)(2,1)}) custom-call(bf16[1024,1792]{1,0:T(8,128)(2,1)} %get-tuple-element.28.p_ref, bf16[1024,1792]{1,0:T(8,128)(2,1)} %get-tuple-element.27.q_ref.q_hbm, bf16[1024,1792]{1,0:T(8,128)(2,1)} %bitcast.4.far_hbm.far_ref, bf16[3,1024,1024]{2,1,0:T(8,128)(2,1)} %get-tuple-element.33.e_ref, ...), custom_call_target="tpu_custom_call" | custom-call | flops 4294967296 | bytes 8388608 | tf_op jit(solution)/shard_map/pallas_call | solution.py:444
  119.9 19.4 %shard_map.143 = (f32[1024,1024]{1,0:T(8,128)}, bf16[1024,1024]{1,0:T(8,128)(2,1)}) custom-call(bf16[1024,1792]{1,0:T(8,128)(2,1)} %get-tuple-element.28.p_ref, bf16[1024,1792]{1,0:T(8,128)(2,1)} %get-tuple-element.27.q_ref.q_hbm, bf16[1024,1792]{1,0:T(8,128)(2,1)} %bitcast.4.far_hbm.far_ref, bf16[3,1024,1024]{2,1,0:T(8,128)(2,1)} %get-tuple-element.33.e_ref, ...), custom_call_target="tpu_custom_call" | custom-call | flops 8589934592 | bytes 16777216 | tf_op jit(solution)/shard_map/pallas_call | solution.py:444
  139.3 3.6 %all-to-all-done.2 = bf16[128,8,1792]{2,1,0:T(8,128)(2,1)} async-done(((bf16[128,8,1792]{2,1,0:T(8,128)(2,1)}), bf16[128,8,1792]{2,1,0:T(8,128)(2,1)}, u32[]{:S(2)}, u32[]{:S(2)}) %all-to-all-start.2) | async-done | bytes 3670048 | tf_op jit(solution)/shard_map/all_to_all | solution.py:32
  142.9 7.3 %shard_map.144 = (f32[1024,256]{1,0:T(8,128)}, f32[1024,512]{1,0:T(8,128)}, f32[1024,1024]{1,0:T(8,128)}) custom-call(s32[1,1024]{1,0:T(1,128)} %select_n.15.place_hbm, bf16[1024,1792]{1,0:T(8,128)(2,1)} %bitcast.8.term_hbm, bf16[1024,256]{1,0:T(8,128)(2,1)} %get-tuple-element.41.part0, bf16[1024,512]{1,0:T(8,128)(2,1)} %get-tuple-element.42.part1, ...), custom_call_target="tpu_custom_call" | custom-call | flops 29360128 | bytes 22020096 | tf_op jit(solution)/shard_map/pallas_call | solution.py:475
Async XLA Ops:
  28.5 5.5 %copy-start.1 = (s32[1024]{0:T(1024)S(1)}, s32[1024]{0:T(1024)}, u32[]{:S(2)}) copy-start(s32[1024]{0:T(1024)} %param.15) | copy-start | bytes 12292
  28.5 51.4 %all-to-all-start.1 = ((bf16[128,8,1792]{2,1,0:T(8,128)(2,1)}), bf16[128,8,1792]{2,1,0:T(8,128)(2,1)}, u32[]{:S(2)}, u32[]{:S(2)}) async-start(bf16[128,8,1792]{2,1,0:T(8,128)(2,1)} %bitcast.10), calls=%async_computation.1 | async-start | bytes 7340032 | tf_op jit(solution)/shard_map/all_to_all | solution.py:32
  91.4 5.6 %copy-start = (s32[128,1,128]{2,1,0:T(1,128)S(1)}, s32[128,1,128]{2,1,0:T(1,128)}, u32[]{:S(2)}) copy-start(s32[128,1,128]{2,1,0:T(1,128)} %all_to_all.15) | copy-start | bytes 196612
  91.4 51.5 %all-to-all-start.2 = ((bf16[128,8,1792]{2,1,0:T(8,128)(2,1)}), bf16[128,8,1792]{2,1,0:T(8,128)(2,1)}, u32[]{:S(2)}, u32[]{:S(2)}) async-start(bf16[128,8,1792]{2,1,0:T(8,128)(2,1)} %bitcast.11), calls=%async_computation.2 | async-start | bytes 7340032 | tf_op jit(solution)/shard_map/all_to_all | solution.py:32

commit v5 on v4

--- a/solution.py
+++ b/solution.py
@@ -49,13 +49,14 @@
     peers = out_ref.shape[0]
     lists, entries = neg_ref.shape
     peer = lax.broadcasted_iota(jnp.int32, (peers, entries), 0)
-    best = jnp.full((peers, 1), -1, jnp.int32)
+    best = jnp.full((peers, entries), -1, jnp.int32)
     for row in range(lists):
         ids = jnp.broadcast_to(neg_ref[row : row + 1, :], (peers, entries))
         local_ids = ids - peer * block_count
         hit = (local_ids >= 0) & (local_ids < block_count)
-        best = jnp.maximum(best, jnp.max(jnp.where(hit, local_ids, -1), axis=1, keepdims=True))
-    out_ref[...] = jnp.broadcast_to(best, out_ref.shape)
+        best = jnp.maximum(best, jnp.where(hit, local_ids, -1))
+    best = jnp.max(best.astype(F32), axis=1, keepdims=True)
+    out_ref[...] = jnp.broadcast_to(best, out_ref.shape).astype(jnp.int32)
 
 
 def heads_kernel(widths, starts, raw0, raw1, raw2, after_ref, out_ref, inv_ref):
@@ -144,8 +145,8 @@
         pltpu.VMEM((8, rows), F32),
         pltpu.VMEM((8, rows), F32),
         pltpu.VMEM((8, rows), F32),
-        pltpu.VMEM((far, rows), BF16),
-        pltpu.VMEM((far, rows), F32),
+        pltpu.VMEM((3, far, rows), BF16),
+        pltpu.VMEM((2, far, rows), F32),
         pltpu.VMEM((far, wide), BF16),
         pltpu.SemaphoreType.DMA((4, 3)),
         pltpu.SemaphoreType.DMA((4, 4)),
@@ -158,7 +159,7 @@
     far_ref, q_ref, bias_ref, tot_ref, spos_ref, scale_ref, loss_ref,
     g_ref, e_v, term_v, in_sems, out_sems,
 ):
-    far, rows = g_ref.shape
+    far, rows = g_ref.shape[1:]
     cols = rows // lists
     chunk = min(256, far)
     order = (0, 1, 2)
@@ -180,7 +181,7 @@
     scale_ref[3:8, :] = jnp.zeros((5, rows), F32)
     loss_ref[3:8, :] = jnp.zeros((5, rows), F32)
     stores = []
-    for k in order:
+    def scores(k):
         span = slice(starts[k], starts[k] + widths[k])
         for load in loads[k]:
             load.wait()
@@ -193,19 +194,18 @@
                 bias = bias_ref[at : at + chunk, b : b + 1]
                 e = jnp.exp2(s * EXP_SCALE + bias)
                 tot = tot + jnp.sum(e, axis=0, keepdims=True)
-                e_v[at : at + chunk, at_q] = e
+                e_v[k % 2, at : at + chunk, at_q] = e
             scale = SHARPNESS / tot
             scale_ref[k : k + 1, at_q] = scale
             loss_ref[k : k + 1, at_q] = jnp.log(tot) - spos_ref[k : k + 1, at_q]
             for at in range(0, far, chunk):
-                g_ref[at : at + chunk, at_q] = (e_v[at : at + chunk, at_q] * scale).astype(BF16)
-        if k == order[-1]:
-            for index, (ref, hbm) in enumerate(((scale_ref, scale_hbm), (loss_ref, loss_hbm))):
-                stores.append(pltpu.make_async_copy(ref, hbm, out_sems.at[3, index]))
-                stores[-1].start()
+                g_ref[k, at : at + chunk, at_q] = (e_v[k % 2, at : at + chunk, at_q] * scale).astype(BF16)
+
+    def send(k):
+        span = slice(starts[k], starts[k] + widths[k])
         for row in range(0, far, chunk):
             here = slice(row, row + chunk)
-            part = jnp.dot(g_ref[here, :], q_ref[:, span], preferred_element_type=F32)
+            part = jnp.dot(g_ref[k, here, :], q_ref[:, span], preferred_element_type=F32)
             unit = far_ref[here, span].astype(F32)
             part = part - unit * jnp.sum(unit * part, axis=1, keepdims=True)
             term_v[here, span] = part.astype(BF16)
@@ -215,6 +215,16 @@
             )
             store.start()
             stores.append(store)
+
+    scores(order[0])
+    send(order[0])
+    scores(order[1])
+    send(order[1])
+    scores(order[2])
+    for index, (ref, hbm) in enumerate(((scale_ref, scale_hbm), (loss_ref, loss_hbm))):
+        stores.append(pltpu.make_async_copy(ref, hbm, out_sems.at[3, index]))
+        stores[-1].start()
+    send(order[2])
     for store in stores:
         store.wait()
 

time: 151 us -> 151 us (level)
  no operation moved by 1% of the time
where the time goes in v5:
time: 151 us; the launch traced here: 150 us
  Pallas kernels  85.1 us (56%)
  waiting for transfers between devices  28.5 us (19%)
  blocking collectives  21.6 us (14%)
  starting transfers between devices  11.1 us (7%)
  other arithmetic  2.39 us (2%)
    pallas_call x3, Pallas kernels, local(): pl.pallas_call(functools.partial(near_kernel, k, lists), grid=(lists,), o...  39.8 us
    all_to_all x2, waiting for transfers between devices, exchange(): return lax.all_to_all(values, AXES, split_axis=0, concat_axis=0, tiled=True)  28.5 us
    all_to_all x1, blocking collectives, exchange(): return lax.all_to_all(values, AXES, split_axis=0, concat_axis=0, tiled=True)  21.6 us
    pallas_call x1, Pallas kernels, local(): pl.pallas_call(functools.partial(far_kernel, widths, starts, lists), out_...  11.4 us
    all_to_all x2, starting transfers between devices, exchange(): return lax.all_to_all(values, AXES, split_axis=0, concat_axis=0, tiled=True)  11.1 us
    pallas_call x1, Pallas kernels, local(): pl.pallas_call(functools.partial(local_kernel, widths, starts, block_coun...  10.3 us
    pallas_call x2, Pallas kernels, heads(): pl.pallas_call(functools.partial(heads_kernel, widths, starts), grid=(4,)...  10.2 us
    pallas_call x1, Pallas kernels, local(): pl.pallas_call(functools.partial(passage_kernel, widths, starts), out_sha...  7.25 us
  transfers between devices with their start and end apart: 2, of which 2 were waited for; matrix products, arithmetic and copies ran while one was open for 2% of the time, Pallas kernels for 40%

profile of v5, /device:TPU:1, one launch (start us, length us, event | category | flops | bytes accessed | tf_op | source)
XLA Modules:
  0.0 150.2 jit_solution(8024493665036659484)
XLA Ops:
  0.6 1.5 shard_map.135
  2.1 21.6 %all_to_all.15 = s32[128,1,128]{2,1,0:T(1,128)} all-to-all(s32[128,1,128]{2,1,0:T(1,128)} %bitcast.15), channel_id=1, replica_groups=mesh['dp'=8,'group'=16] {'dp','group'}, dimensions={0} | all-to-all | bytes 131072 | tf_op jit(solution)/shard_map/all_to_all | solution.py:32
  23.7 4.7 %shard_map.136.after_ref = bf16[1024,1792]{1,0:T(8,128)(2,1)} custom-call(s32[128,128]{1,0:T(8,128)} %bitcast.12, bf16[1024,256]{1,0:T(8,128)(2,1)} %p_raw_ref.3, bf16[1024,512]{1,0:T(8,128)(2,1)} %p_raw_ref.4, bf16[1024,1024]{1,0:T(8,128)(2,1)} %p_raw_ref.5), custom_call_target="tpu_custom_call" | custom-call | flops 7340032 | bytes 7340032 | tf_op jit(solution)/shard_map/pallas_call | solution.py:395
  28.4 0.0 copy-start.1
  28.4 5.5 %all-to-all-start.1 = ((bf16[128,8,1792]{2,1,0:T(8,128)(2,1)}), bf16[128,8,1792]{2,1,0:T(8,128)(2,1)}, u32[]{:S(2)}, u32[]{:S(2)}) async-start(bf16[128,8,1792]{2,1,0:T(8,128)(2,1)} %bitcast.10), calls=%async_computation.1 | async-start | bytes 7340032 | tf_op jit(solution)/shard_map/all_to_all | solution.py:32
  33.9 0.0 copy-done.1
  33.9 0.6 broadcast_subtract_fusion
  34.5 5.1 %shard_map.138 = (bf16[1024,1792]{1,0:T(8,128)(2,1)}, f32[1024,128]{1,0:T(8,128)}) custom-call(bf16[1024,256]{1,0:T(8,128)(2,1)} %p_raw_ref.3, bf16[1024,512]{1,0:T(8,128)(2,1)} %p_raw_ref.4, bf16[1024,1024]{1,0:T(8,128)(2,1)} %p_raw_ref.5, bf16[1024,1792]{1,0:T(8,128)(2,1)} %shard_map.136.after_ref), custom_call_target="tpu_custom_call" | custom-call | flops 7340032 | bytes 7340032 | tf_op jit(solution)/shard_map/pallas_call | solution.py:385
  39.6 5.1 %shard_map.137 = (bf16[1024,1792]{1,0:T(8,128)(2,1)}, f32[1024,128]{1,0:T(8,128)}) custom-call(bf16[1024,256]{1,0:T(8,128)(2,1)} %raw_ref.3, bf16[1024,512]{1,0:T(8,128)(2,1)} %raw_ref.4, bf16[1024,1024]{1,0:T(8,128)(2,1)} %raw_ref.5, bf16[1024,1792]{1,0:T(8,128)(2,1)} %shard_map.136.after_ref), custom_call_target="tpu_custom_call" | custom-call | flops 7340032 | bytes 7340032 | tf_op jit(solution)/shard_map/pallas_call | solution.py:385
  44.7 10.3 %shard_map.139 = (f32[8,1024]{1,0:T(8,128)}, f32[8,1024]{1,0:T(8,128)}, f32[1024,128]{1,0:T(8,128)}, bf16[3,1024,1024]{2,1,0:T(8,128)(2,1)}) custom-call(bf16[1024,1792]{1,0:T(8,128)(2,1)} %get-tuple-element.28.p_ref, bf16[1024,1792]{1,0:T(8,128)(2,1)} %get-tuple-element.27.q_ref.q_hbm, s32[1,1024]{1,0:T(1,128)} %bitcast.16, s32[4,127]{1,0:T(4,128)} %neg_ref.3), custom_call_target="tpu_custom_call" | custom-call | flops 3758096384 | bytes 7340032 | tf_op jit(solution)/shard_map/pallas_call | solution.py:412
  54.9 24.9 %all-to-all-done.1 = bf16[128,8,1792]{2,1,0:T(8,128)(2,1)} async-done(((bf16[128,8,1792]{2,1,0:T(8,128)(2,1)}), bf16[128,8,1792]{2,1,0:T(8,128)(2,1)}, u32[]{:S(2)}, u32[]{:S(2)}) %all-to-all-start.1) | async-done | bytes 3670048 | tf_op jit(solution)/shard_map/all_to_all | solution.py:32
  79.8 11.4 %shard_map.140 = (bf16[1024,1792]{1,0:T(8,128)(2,1)}, f32[8,1024]{1,0:T(8,128)}, f32[8,1024]{1,0:T(8,128)}) custom-call(bf16[1024,1792]{1,0:T(8,128)(2,1)} %bitcast.4.far_hbm.far_ref, bf16[1024,1792]{1,0:T(8,128)(2,1)} %get-tuple-element.27.q_ref.q_hbm, f32[1024,128]{1,0:T(8,128)} %get-tuple-element.29.bias_hbm.bias_ref, ...), custom_call_target="tpu_custom_call" | custom-call | flops 7516192768 | bytes 11010048 | tf_op jit(solution)/shard_map/pallas_call | solution.py:437
  91.3 0.0 copy-start
  91.3 5.6 %all-to-all-start.2 = ((bf16[128,8,1792]{2,1,0:T(8,128)(2,1)}), bf16[128,8,1792]{2,1,0:T(8,128)(2,1)}, u32[]{:S(2)}, u32[]{:S(2)}) async-start(bf16[128,8,1792]{2,1,0:T(8,128)(2,1)} %bitcast.11), calls=%async_computation.2 | async-start | bytes 7340032 | tf_op jit(solution)/shard_map/all_to_all | solution.py:32
  96.9 0.0 copy-done
  96.9 0.1 multiply_reduce_fusion
  97.0 0.1 compare_reduce_fusion
  97.1 0.1 add_select_fusion
  97.2 0.7 select_n.15.place_hbm
  97.9 8.6 %shard_map.141 = (f32[1024,256]{1,0:T(8,128)}, bf16[1024,256]{1,0:T(8,128)(2,1)}) custom-call(bf16[1024,1792]{1,0:T(8,128)(2,1)} %get-tuple-element.28.p_ref, bf16[1024,1792]{1,0:T(8,128)(2,1)} %get-tuple-element.27.q_ref.q_hbm, bf16[1024,1792]{1,0:T(8,128)(2,1)} %bitcast.4.far_hbm.far_ref, bf16[3,1024,1024]{2,1,0:T(8,128)(2,1)} %get-tuple-element.33.e_ref, ...), custom_call_target="tpu_custom_call" | custom-call | flops 2147483648 | bytes 4194304 | tf_op jit(solution)/shard_map/pallas_call | solution.py:454
  106.5 1.5 slice_add_fusion
  108.0 11.8 %shard_map.142 = (f32[1024,512]{1,0:T(8,128)}, bf16[1024,512]{1,0:T(8,128)(2,1)}) custom-call(bf16[1024,1792]{1,0:T(8,128)(2,1)} %get-tuple-element.28.p_ref, bf16[1024,1792]{1,0:T(8,128)(2,1)} %get-tuple-element.27.q_ref.q_hbm, bf16[1024,1792]{1,0:T(8,128)(2,1)} %bitcast.4.far_hbm.far_ref, bf16[3,1024,1024]{2,1,0:T(8,128)(2,1)} %get-tuple-element.33.e_ref, ...), custom_call_target="tpu_custom_call" | custom-call | flops 4294967296 | bytes 8388608 | tf_op jit(solution)/shard_map/pallas_call | solution.py:454
  119.8 19.4 %shard_map.143 = (f32[1024,1024]{1,0:T(8,128)}, bf16[1024,1024]{1,0:T(8,128)(2,1)}) custom-call(bf16[1024,1792]{1,0:T(8,128)(2,1)} %get-tuple-element.28.p_ref, bf16[1024,1792]{1,0:T(8,128)(2,1)} %get-tuple-element.27.q_ref.q_hbm, bf16[1024,1792]{1,0:T(8,128)(2,1)} %bitcast.4.far_hbm.far_ref, bf16[3,1024,1024]{2,1,0:T(8,128)(2,1)} %get-tuple-element.33.e_ref, ...), custom_call_target="tpu_custom_call" | custom-call | flops 8589934592 | bytes 16777216 | tf_op jit(solution)/shard_map/pallas_call | solution.py:454
  139.2 3.6 %all-to-all-done.2 = bf16[128,8,1792]{2,1,0:T(8,128)(2,1)} async-done(((bf16[128,8,1792]{2,1,0:T(8,128)(2,1)}), bf16[128,8,1792]{2,1,0:T(8,128)(2,1)}, u32[]{:S(2)}, u32[]{:S(2)}) %all-to-all-start.2) | async-done | bytes 3670048 | tf_op jit(solution)/shard_map/all_to_all | solution.py:32
  142.8 7.3 %shard_map.144 = (f32[1024,256]{1,0:T(8,128)}, f32[1024,512]{1,0:T(8,128)}, f32[1024,1024]{1,0:T(8,128)}) custom-call(s32[1,1024]{1,0:T(1,128)} %select_n.15.place_hbm, bf16[1024,1792]{1,0:T(8,128)(2,1)} %bitcast.8.term_hbm, bf16[1024,256]{1,0:T(8,128)(2,1)} %get-tuple-element.41.part0, bf16[1024,512]{1,0:T(8,128)(2,1)} %get-tuple-element.42.part1, ...), custom_call_target="tpu_custom_call" | custom-call | flops 29360128 | bytes 22020096 | tf_op jit(solution)/shard_map/pallas_call | solution.py:485
Async XLA Ops:
  28.4 5.5 %copy-start.1 = (s32[1024]{0:T(1024)S(1)}, s32[1024]{0:T(1024)}, u32[]{:S(2)}) copy-start(s32[1024]{0:T(1024)} %param.15) | copy-start | bytes 12292
  28.4 51.4 %all-to-all-start.1 = ((bf16[128,8,1792]{2,1,0:T(8,128)(2,1)}), bf16[128,8,1792]{2,1,0:T(8,128)(2,1)}, u32[]{:S(2)}, u32[]{:S(2)}) async-start(bf16[128,8,1792]{2,1,0:T(8,128)(2,1)} %bitcast.10), calls=%async_computation.1 | async-start | bytes 7340032 | tf_op jit(solution)/shard_map/all_to_all | solution.py:32
  91.3 5.6 %copy-start = (s32[128,1,128]{2,1,0:T(1,128)S(1)}, s32[128,1,128]{2,1,0:T(1,128)}, u32[]{:S(2)}) copy-start(s32[128,1,128]{2,1,0:T(1,128)} %all_to_all.15) | copy-start | bytes 196612
  91.3 51.5 %all-to-all-start.2 = ((bf16[128,8,1792]{2,1,0:T(8,128)(2,1)}), bf16[128,8,1792]{2,1,0:T(8,128)(2,1)}, u32[]{:S(2)}, u32[]{:S(2)}) async-start(bf16[128,8,1792]{2,1,0:T(8,128)(2,1)} %bitcast.11), calls=%async_computation.2 | async-start | bytes 7340032 | tf_op jit(solution)/shard_map/all_to_all | solution.py:32

commit v6 on v5

--- a/solution.py
+++ b/solution.py
@@ -133,14 +133,14 @@
             hit = (local_ids >= 0) & (local_ids < block_count)
             listed = jnp.max(jnp.where(hit, 1.0, 0.0), axis=1, keepdims=True)
             bias = jnp.where((lane == b) & (listed > 0.0), 0.0, bias)
-        bias_ref[...] = bias
+        bias_ref[...] = bias.astype(BF16)
 
 
 def far_scratch(far, rows, wide):
     return [
         pltpu.VMEM((far, wide), BF16),
         pltpu.VMEM((rows, wide), BF16),
-        pltpu.VMEM((far, LANES), F32),
+        pltpu.VMEM((far, LANES), BF16),
         pltpu.VMEM((8, rows), F32),
         pltpu.VMEM((8, rows), F32),
         pltpu.VMEM((8, rows), F32),
@@ -191,7 +191,7 @@
             tot = tot_ref[k : k + 1, at_q]
             for at in range(0, far, chunk):
                 s = lax.dot_general(far_ref[at : at + chunk, span], q, NT, preferred_element_type=F32)
-                bias = bias_ref[at : at + chunk, b : b + 1]
+                bias = bias_ref[at : at + chunk, :].astype(F32)[:, b : b + 1]
                 e = jnp.exp2(s * EXP_SCALE + bias)
                 tot = tot + jnp.sum(e, axis=0, keepdims=True)
                 e_v[k % 2, at : at + chunk, at_q] = e
@@ -205,7 +205,13 @@
         span = slice(starts[k], starts[k] + widths[k])
         for row in range(0, far, chunk):
             here = slice(row, row + chunk)
-            part = jnp.dot(g_ref[k, here, :], q_ref[:, span], preferred_element_type=F32)
+            part = jnp.concatenate(
+                [
+                    jnp.dot(g_ref[k, here, :], q_ref[:, at : at + 256], preferred_element_type=F32)
+                    for at in range(starts[k], starts[k] + widths[k], 256)
+                ],
+                axis=1,
+            )
             unit = far_ref[here, span].astype(F32)
             part = part - unit * jnp.sum(unit * part, axis=1, keepdims=True)
             term_v[here, span] = part.astype(BF16)
@@ -250,7 +256,7 @@
     parts = []
     for at in range(0, far, chunk):
         s = lax.dot_general(far_ref[at : at + chunk, :], q, NT, preferred_element_type=F32)
-        bias = jnp.sum(jnp.where(lane == step, bias_ref[at : at + chunk, :], 0.0), axis=1, keepdims=True)
+        bias = jnp.sum(jnp.where(lane == step, bias_ref[at : at + chunk, :].astype(F32), 0.0), axis=1, keepdims=True)
         parts.append((jnp.exp2(s * EXP_SCALE + bias) * scale).astype(BF16))
     dq = lax.dot_general(
         jnp.concatenate(parts, axis=0), far_ref[...], TN, preferred_element_type=F32
@@ -415,7 +421,7 @@
         out_shape=(
             shape((8, rows), F32),
             shape((8, rows), F32),
-            shape((far, LANES), F32),
+            shape((far, LANES), BF16),
             shape((3, rows, rows), BF16),
         ),
         in_specs=[

time: 151 us -> 151 us (level)
  no operation moved by 1% of the time
where the time goes in v6:
time: 151 us; the launch traced here: 150 us
  Pallas kernels  84.8 us (56%)
  waiting for transfers between devices  28.9 us (19%)
  blocking collectives  21.6 us (14%)
  starting transfers between devices  11 us (7%)
  other arithmetic  2.39 us (2%)
    pallas_call x3, Pallas kernels, local(): pl.pallas_call(functools.partial(near_kernel, k, lists), grid=(lists,), o...  39.5 us
    all_to_all x2, waiting for transfers between devices, exchange(): return lax.all_to_all(values, AXES, split_axis=0, concat_axis=0, tiled=True)  28.9 us
    all_to_all x1, blocking collectives, exchange(): return lax.all_to_all(values, AXES, split_axis=0, concat_axis=0, tiled=True)  21.6 us
    pallas_call x1, Pallas kernels, local(): pl.pallas_call(functools.partial(far_kernel, widths, starts, lists), out_...  11.5 us
    all_to_all x2, starting transfers between devices, exchange(): return lax.all_to_all(values, AXES, split_axis=0, concat_axis=0, tiled=True)  11 us
    pallas_call x1, Pallas kernels, local(): pl.pallas_call(functools.partial(local_kernel, widths, starts, block_coun...  10.2 us
    pallas_call x2, Pallas kernels, heads(): pl.pallas_call(functools.partial(heads_kernel, widths, starts), grid=(4,)...  10.2 us
    pallas_call x1, Pallas kernels, local(): pl.pallas_call(functools.partial(passage_kernel, widths, starts), out_sha...  7.25 us
  transfers between devices with their start and end apart: 2, of which 2 were waited for; matrix products, arithmetic and copies ran while one was open for 2% of the time, Pallas kernels for 40%

profile of v6, /device:TPU:1, one launch (start us, length us, event | category | flops | bytes accessed | tf_op | source)
XLA Modules:
  0.0 150.3 jit_solution(12449417570931853177)
XLA Ops:
  0.6 1.5 shard_map.135
  2.1 21.6 %all_to_all.15 = s32[128,1,128]{2,1,0:T(1,128)} all-to-all(s32[128,1,128]{2,1,0:T(1,128)} %bitcast.15), channel_id=1, replica_groups=mesh['dp'=8,'group'=16] {'dp','group'}, dimensions={0} | all-to-all | bytes 131072 | tf_op jit(solution)/shard_map/all_to_all | solution.py:32
  23.7 4.7 %shard_map.136.after_ref = bf16[1024,1792]{1,0:T(8,128)(2,1)} custom-call(s32[128,128]{1,0:T(8,128)} %bitcast.12, bf16[1024,256]{1,0:T(8,128)(2,1)} %p_raw_ref.3, bf16[1024,512]{1,0:T(8,128)(2,1)} %p_raw_ref.4, bf16[1024,1024]{1,0:T(8,128)(2,1)} %p_raw_ref.5), custom_call_target="tpu_custom_call" | custom-call | flops 7340032 | bytes 7340032 | tf_op jit(solution)/shard_map/pallas_call | solution.py:401
  28.4 0.0 copy-start.1
  28.4 5.5 %all-to-all-start.1 = ((bf16[128,8,1792]{2,1,0:T(8,128)(2,1)}), bf16[128,8,1792]{2,1,0:T(8,128)(2,1)}, u32[]{:S(2)}, u32[]{:S(2)}) async-start(bf16[128,8,1792]{2,1,0:T(8,128)(2,1)} %bitcast.10), calls=%async_computation.1 | async-start | bytes 7340032 | tf_op jit(solution)/shard_map/all_to_all | solution.py:32
  33.9 0.0 copy-done.1
  33.9 0.6 broadcast_subtract_fusion
  34.5 5.1 %shard_map.138 = (bf16[1024,1792]{1,0:T(8,128)(2,1)}, f32[1024,128]{1,0:T(8,128)}) custom-call(bf16[1024,256]{1,0:T(8,128)(2,1)} %p_raw_ref.3, bf16[1024,512]{1,0:T(8,128)(2,1)} %p_raw_ref.4, bf16[1024,1024]{1,0:T(8,128)(2,1)} %p_raw_ref.5, bf16[1024,1792]{1,0:T(8,128)(2,1)} %shard_map.136.after_ref), custom_call_target="tpu_custom_call" | custom-call | flops 7340032 | bytes 7340032 | tf_op jit(solution)/shard_map/pallas_call | solution.py:391
  39.6 5.1 %shard_map.137 = (bf16[1024,1792]{1,0:T(8,128)(2,1)}, f32[1024,128]{1,0:T(8,128)}) custom-call(bf16[1024,256]{1,0:T(8,128)(2,1)} %raw_ref.3, bf16[1024,512]{1,0:T(8,128)(2,1)} %raw_ref.4, bf16[1024,1024]{1,0:T(8,128)(2,1)} %raw_ref.5, bf16[1024,1792]{1,0:T(8,128)(2,1)} %shard_map.136.after_ref), custom_call_target="tpu_custom_call" | custom-call | flops 7340032 | bytes 7340032 | tf_op jit(solution)/shard_map/pallas_call | solution.py:391
  44.7 10.2 %shard_map.139 = (f32[8,1024]{1,0:T(8,128)}, f32[8,1024]{1,0:T(8,128)}, bf16[1024,128]{1,0:T(8,128)(2,1)}, bf16[3,1024,1024]{2,1,0:T(8,128)(2,1)}) custom-call(bf16[1024,1792]{1,0:T(8,128)(2,1)} %get-tuple-element.28.p_ref, bf16[1024,1792]{1,0:T(8,128)(2,1)} %get-tuple-element.27.q_ref.q_hbm, s32[1,1024]{1,0:T(1,128)} %bitcast.16, s32[4,127]{1,0:T(4,128)} %neg_ref.3), custom_call_target="tpu_custom_call" | custom-call | flops 3758096384 | bytes 7340032 | tf_op jit(solution)/shard_map/pallas_call | solution.py:418
  54.8 25.0 %all-to-all-done.1 = bf16[128,8,1792]{2,1,0:T(8,128)(2,1)} async-done(((bf16[128,8,1792]{2,1,0:T(8,128)(2,1)}), bf16[128,8,1792]{2,1,0:T(8,128)(2,1)}, u32[]{:S(2)}, u32[]{:S(2)}) %all-to-all-start.1) | async-done | bytes 3670048 | tf_op jit(solution)/shard_map/all_to_all | solution.py:32
  79.8 11.5 %shard_map.140 = (bf16[1024,1792]{1,0:T(8,128)(2,1)}, f32[8,1024]{1,0:T(8,128)}, f32[8,1024]{1,0:T(8,128)}) custom-call(bf16[1024,1792]{1,0:T(8,128)(2,1)} %bitcast.4.far_hbm.far_ref, bf16[1024,1792]{1,0:T(8,128)(2,1)} %get-tuple-element.27.q_ref.q_hbm, bf16[1024,128]{1,0:T(8,128)(2,1)} %get-tuple-element.29.bias_hbm.bias_ref, ...), custom_call_target="tpu_custom_call" | custom-call | flops 7516192768 | bytes 11010048 | tf_op jit(solution)/shard_map/pallas_call | solution.py:443
  91.3 0.0 copy-start
  91.4 5.6 %all-to-all-start.2 = ((bf16[128,8,1792]{2,1,0:T(8,128)(2,1)}), bf16[128,8,1792]{2,1,0:T(8,128)(2,1)}, u32[]{:S(2)}, u32[]{:S(2)}) async-start(bf16[128,8,1792]{2,1,0:T(8,128)(2,1)} %bitcast.11), calls=%async_computation.2 | async-start | bytes 7340032 | tf_op jit(solution)/shard_map/all_to_all | solution.py:32
  97.0 0.0 copy-done
  97.0 0.1 multiply_reduce_fusion
  97.1 0.1 compare_reduce_fusion
  97.2 0.1 add_select_fusion
  97.3 0.7 select_n.15.place_hbm
  98.0 8.6 %shard_map.141 = (f32[1024,256]{1,0:T(8,128)}, bf16[1024,256]{1,0:T(8,128)(2,1)}) custom-call(bf16[1024,1792]{1,0:T(8,128)(2,1)} %get-tuple-element.28.p_ref, bf16[1024,1792]{1,0:T(8,128)(2,1)} %get-tuple-element.27.q_ref.q_hbm, bf16[1024,1792]{1,0:T(8,128)(2,1)} %bitcast.4.far_hbm.far_ref, bf16[3,1024,1024]{2,1,0:T(8,128)(2,1)} %get-tuple-element.33.e_ref, ...), custom_call_target="tpu_custom_call" | custom-call | flops 2147483648 | bytes 4194304 | tf_op jit(solution)/shard_map/pallas_call | solution.py:460
  106.6 1.5 slice_add_fusion
  108.0 11.7 %shard_map.142 = (f32[1024,512]{1,0:T(8,128)}, bf16[1024,512]{1,0:T(8,128)(2,1)}) custom-call(bf16[1024,1792]{1,0:T(8,128)(2,1)} %get-tuple-element.28.p_ref, bf16[1024,1792]{1,0:T(8,128)(2,1)} %get-tuple-element.27.q_ref.q_hbm, bf16[1024,1792]{1,0:T(8,128)(2,1)} %bitcast.4.far_hbm.far_ref, bf16[3,1024,1024]{2,1,0:T(8,128)(2,1)} %get-tuple-element.33.e_ref, ...), custom_call_target="tpu_custom_call" | custom-call | flops 4294967296 | bytes 8388608 | tf_op jit(solution)/shard_map/pallas_call | solution.py:460
  119.7 19.2 %shard_map.143 = (f32[1024,1024]{1,0:T(8,128)}, bf16[1024,1024]{1,0:T(8,128)(2,1)}) custom-call(bf16[1024,1792]{1,0:T(8,128)(2,1)} %get-tuple-element.28.p_ref, bf16[1024,1792]{1,0:T(8,128)(2,1)} %get-tuple-element.27.q_ref.q_hbm, bf16[1024,1792]{1,0:T(8,128)(2,1)} %bitcast.4.far_hbm.far_ref, bf16[3,1024,1024]{2,1,0:T(8,128)(2,1)} %get-tuple-element.33.e_ref, ...), custom_call_target="tpu_custom_call" | custom-call | flops 8589934592 | bytes 16777216 | tf_op jit(solution)/shard_map/pallas_call | solution.py:460
  139.0 3.9 %all-to-all-done.2 = bf16[128,8,1792]{2,1,0:T(8,128)(2,1)} async-done(((bf16[128,8,1792]{2,1,0:T(8,128)(2,1)}), bf16[128,8,1792]{2,1,0:T(8,128)(2,1)}, u32[]{:S(2)}, u32[]{:S(2)}) %all-to-all-start.2) | async-done | bytes 3670048 | tf_op jit(solution)/shard_map/all_to_all | solution.py:32
  142.9 7.3 %shard_map.144 = (f32[1024,256]{1,0:T(8,128)}, f32[1024,512]{1,0:T(8,128)}, f32[1024,1024]{1,0:T(8,128)}) custom-call(s32[1,1024]{1,0:T(1,128)} %select_n.15.place_hbm, bf16[1024,1792]{1,0:T(8,128)(2,1)} %bitcast.8.term_hbm, bf16[1024,256]{1,0:T(8,128)(2,1)} %get-tuple-element.41.part0, bf16[1024,512]{1,0:T(8,128)(2,1)} %get-tuple-element.42.part1, ...), custom_call_target="tpu_custom_call" | custom-call | flops 29360128 | bytes 22020096 | tf_op jit(solution)/shard_map/pallas_call | solution.py:491
Async XLA Ops:
  28.4 5.5 %copy-start.1 = (s32[1024]{0:T(1024)S(1)}, s32[1024]{0:T(1024)}, u32[]{:S(2)}) copy-start(s32[1024]{0:T(1024)} %param.15) | copy-start | bytes 12292
  28.4 51.4 %all-to-all-start.1 = ((bf16[128,8,1792]{2,1,0:T(8,128)(2,1)}), bf16[128,8,1792]{2,1,0:T(8,128)(2,1)}, u32[]{:S(2)}, u32[]{:S(2)}) async-start(bf16[128,8,1792]{2,1,0:T(8,128)(2,1)} %bitcast.10), calls=%async_computation.1 | async-start | bytes 7340032 | tf_op jit(solution)/shard_map/all_to_all | solution.py:32
  91.3 5.6 %copy-start = (s32[128,1,128]{2,1,0:T(1,128)S(1)}, s32[128,1,128]{2,1,0:T(1,128)}, u32[]{:S(2)}) copy-start(s32[128,1,128]{2,1,0:T(1,128)} %all_to_all.15) | copy-start | bytes 196612
  91.4 51.5 %all-to-all-start.2 = ((bf16[128,8,1792]{2,1,0:T(8,128)(2,1)}), bf16[128,8,1792]{2,1,0:T(8,128)(2,1)}, u32[]{:S(2)}, u32[]{:S(2)}) async-start(bf16[128,8,1792]{2,1,0:T(8,128)(2,1)} %bitcast.11), calls=%async_computation.2 | async-start | bytes 7340032 | tf_op jit(solution)/shard_map/all_to_all | solution.py:32
